TPU v7x, 512 devices: a whole 4x8x8 slice. The times are simulated.
512 devices in a mesh: dp: 32 (over x, y), seq: 16 (over z, core).
Axes of the slice: x: 4, y: 8, z: 8, core: 2. Of those that a mesh axis runs over, the one named last changes fastest.
Arguments:
- queries: bfloat16 [65536, 2048], P(('dp', 'seq')), may hold values from -6 to 6
- keys: bfloat16 [65536, 2048], P(('dp', 'seq')), may hold values from -6 to 6
- values: bfloat16 [65536, 2048], P(('dp', 'seq')), may hold values from -6 to 6
- text_kv: bfloat16 [256, 256, 2, 2048], P('dp', None, None, 'seq'), may hold values from -6 to 6
- text_lengths: int32 [256], P('dp'), may hold values from 1 to 256
- clip_lengths: int32 [32, 8], P('dp'), may hold values from 1 to 512, 2048 in all within a row
- timesteps: int32 [256], P('dp'), may hold values from 0 to 999
- mod_weight: bfloat16 [256, 4096], replicated, may hold values from -0.375 to 0.375
- final_weight: bfloat16 [2048, 64], replicated, may hold values from -0.125 to 0.125
- noise: float32 [65536, 64], P(('dp', 'seq')), may hold values from -6 to 6
- clean: float32 [65536, 64], P(('dp', 'seq')), may hold values from -12 to 12
- report_order: int32 [256], P('dp'), may hold values from 0 to 255, each once
Outputs:
- scores: float32 [256], P('dp')
Inputs may be any that keep to these rules, and one draw needn't show every extreme that they name: Each row of clip_lengths sums to 2048, and its largest entry is exactly 512.
All inputs are finite; a program needn't handle non-finite values.
Results may differ from a plain program's by a relative error of at most 0.00055.
Values may be sent and summed in bfloat16 or wider, within the bound.
A program may use at most 64 MiB of HBM per device.

v0:
```python
import math

import jax
import jax.numpy as jnp
from jax import lax
from jax.sharding import PartitionSpec as P

HEAD_DIM = 128
FREQ = 256


eps_norm = 1e-06


def step_embedding(timesteps):
    half_width = FREQ // 2
    frequency = jnp.exp(-math.log(10000.0) * jnp.arange(half_width, dtype=jnp.float32) / half_width)
    angles = timesteps.astype(jnp.float32)[:, None] * frequency[None, :]
    return jnp.concatenate([jnp.cos(angles), jnp.sin(angles)], axis=1)


def clip_index(lengths, row_total):
    clip_ends = jnp.cumsum(lengths)
    places = jnp.arange(row_total, dtype=jnp.int32)
    return jnp.sum((places[:, None] >= clip_ends[None, :]).astype(jnp.int32), axis=1)


def attend_block(query_block, key_rows, value_rows, live_mask):
    row_count = query_block.shape[0]
    heads_here = query_block.shape[1] // HEAD_DIM
    query_split = query_block.reshape(row_count, heads_here, HEAD_DIM)
    key_split = key_rows.reshape(key_rows.shape[0], heads_here, HEAD_DIM)
    value_split = value_rows.reshape(value_rows.shape[0], heads_here, HEAD_DIM)
    score_rows = jnp.einsum(
        "qhd,khd->hqk", query_split, key_split, preferred_element_type=jnp.float32
    ) * (1.0 / math.sqrt(HEAD_DIM))
    score_rows = jnp.where(live_mask[None], score_rows, -jnp.inf)
    row_top = jnp.max(score_rows, axis=2, keepdims=True)
    weights = jnp.exp(score_rows - row_top)
    weights = (weights / jnp.sum(weights, axis=2, keepdims=True)).astype(jnp.bfloat16)
    mixed_out = jnp.einsum("hqk,khd->qhd", weights, value_split, preferred_element_type=jnp.float32)
    return mixed_out.reshape(row_count, heads_here * HEAD_DIM).astype(jnp.bfloat16)


def per_device(
    queries,
    keys,
    values,
    text_kv,
    text_lengths,
    clip_lengths,
    timesteps,
    mod_weight,
    final_weight,
    noise,
    clean,
    report_order,
):
    tok_dev = queries.shape[0]
    feat_width = queries.shape[1]
    seq_count = lax.axis_size("seq")
    seq_rank = lax.axis_index("seq")
    query_heads, key_heads, value_heads = (
        lax.all_to_all(queries, "seq", split_axis=1, concat_axis=0, tiled=True),
        lax.all_to_all(keys, "seq", split_axis=1, concat_axis=0, tiled=True),
        lax.all_to_all(values, "seq", split_axis=1, concat_axis=0, tiled=True),
    )
    group_rows = tok_dev * seq_count
    local_width = query_heads.shape[1]
    block_rows = min(512, group_rows)
    lengths = clip_lengths[0]
    clips_here = lengths.shape[0]
    clip_of = clip_index(lengths, group_rows)
    clip_slots = jnp.arange(clips_here, dtype=jnp.int32)
    text_len = text_kv.shape[1]
    text_slots = jnp.arange(clips_here * text_len, dtype=jnp.int32)
    text_clip = text_slots // text_len
    text_live = text_slots % text_len < text_lengths[text_clip]
    text_keys = text_kv[:, :, 0, :].reshape(clips_here * text_len, local_width)
    text_values = text_kv[:, :, 1, :].reshape(clips_here * text_len, local_width)

    def one_block(block_index):
        first_row = block_index * block_rows
        query_block = lax.dynamic_slice_in_dim(query_heads, first_row, block_rows, 0)
        block_clip = lax.dynamic_slice_in_dim(clip_of, first_row, block_rows, 0)
        live_mask = jnp.concatenate(
            [
                block_clip[:, None] == clip_of[None, :],
                (block_clip[:, None] == text_clip[None, :]) & text_live[None, :],
            ],
            axis=1,
        )
        return attend_block(
            query_block,
            jnp.concatenate([key_heads, text_keys], axis=0),
            jnp.concatenate([value_heads, text_values], axis=0),
            live_mask,
        )

    attended = lax.map(one_block, jnp.arange(group_rows // block_rows, dtype=jnp.int32)).reshape(
        group_rows, local_width
    )
    activated = jax.nn.silu(step_embedding(timesteps)).astype(jnp.bfloat16)
    modulation = jnp.dot(activated, mod_weight, preferred_element_type=jnp.float32)
    tok_clip = lax.dynamic_slice_in_dim(clip_of, seq_rank * tok_dev, tok_dev, 0)
    token_picks = (tok_clip[:, None] == clip_slots[None, :]).astype(jnp.float32)
    gathered = lax.all_to_all(attended, "seq", split_axis=0, concat_axis=1, tiled=True)
    tok_mods = jnp.dot(token_picks, modulation, precision=lax.Precision.HIGHEST)
    values_full = gathered.astype(jnp.float32)
    center = jnp.mean(values_full, axis=1, keepdims=True)
    spread = jnp.mean(values_full * values_full, axis=1, keepdims=True) - center * center
    normed = (values_full - center) * lax.rsqrt(spread + eps_norm)
    modulated = normed * (1.0 + tok_mods[:, feat_width:]) + tok_mods[:, :feat_width]
    predicted = jnp.dot(
        modulated, final_weight.astype(jnp.float32), precision=lax.Precision.HIGHEST
    )
    difference = predicted - (noise - clean)
    error_rows = jnp.mean(difference * difference, axis=1)
    clip_partial = jnp.sum(token_picks * error_rows[:, None], axis=0)
    clip_sizes = lengths.astype(jnp.float32)
    clip_totals = lax.psum(clip_partial, "seq")
    all_losses = lax.all_gather(clip_totals / clip_sizes, "dp", axis=0, tiled=True)
    loss_slots = jnp.arange(all_losses.shape[0], dtype=jnp.int32)
    return jnp.sum(
        jnp.where(report_order[:, None] == loss_slots[None, :], all_losses[None, :], 0.0), axis=1
    )


def solution(mesh):
    in_specs = (
        P(("dp", "seq"), None),
        P(("dp", "seq"), None),
        P(("dp", "seq"), None),
        P("dp", None, None, "seq"),
        P("dp"),
        P("dp", None),
        P("dp"),
        P(),
        P(),
        P(("dp", "seq"), None),
        P(("dp", "seq"), None),
        P("dp"),
    )
    out_specs = P("dp")
    return jax.shard_map(
        per_device, mesh=mesh, in_specs=in_specs, out_specs=out_specs, check_vma=False
    )
```

profile of v0, /device:TPU:8, one launch (start us, length us, event | category | flops | bytes accessed | tf_op | source)
XLA Modules:
  0.0 250.3 jit_solution(14884609257005727516)
XLA Ops:
  0.0 2.1 copy_bitcast_fusion.1
  2.1 10.5 %all-to-all-start.1 = ((bf16[128,16,128]{2,0,1:T(8,128)(2,1)}), bf16[128,16,128]{2,0,1:T(8,128)(2,1)}, u32[]{:S(2)}, u32[]{:S(2)}) async-start(bf16[128,16,128]{2,0,1:T(8,128)(2,1)} %copy_bitcast_fusion.1), calls=%async_computation.1 | async-start | bytes 1048576 | tf_op jit(solution)/shard_map/all_to_all | solution.py:65
  12.6 2.0 copy_bitcast_fusion
  14.6 14.1 %all-to-all-done.1 = bf16[128,16,128]{2,0,1:T(8,128)(2,1)} async-done(((bf16[128,16,128]{2,0,1:T(8,128)(2,1)}), bf16[128,16,128]{2,0,1:T(8,128)(2,1)}, u32[]{:S(2)}, u32[]{:S(2)}) %all-to-all-start.1) | async-done | bytes 524320 | tf_op jit(solution)/shard_map/all_to_all | solution.py:65
  28.7 4.3 %all-to-all-start.2 = ((bf16[128,16,128]{2,0,1:T(8,128)(2,1)}), bf16[128,16,128]{2,0,1:T(8,128)(2,1)}, u32[]{:S(2)}, u32[]{:S(2)}) async-start(bf16[128,16,128]{2,0,1:T(8,128)(2,1)} %copy_bitcast_fusion), calls=%async_computation.2 | async-start | bytes 1048576 | tf_op jit(solution)/shard_map/all_to_all | solution.py:66
  33.2 2.0 copy_bitcast_fusion.2
  35.2 2.5 fusion.39
  37.7 11.4 %all-to-all-done.2 = bf16[128,16,128]{2,0,1:T(8,128)(2,1)} async-done(((bf16[128,16,128]{2,0,1:T(8,128)(2,1)}), bf16[128,16,128]{2,0,1:T(8,128)(2,1)}, u32[]{:S(2)}, u32[]{:S(2)}) %all-to-all-start.2) | async-done | bytes 524320 | tf_op jit(solution)/shard_map/all_to_all | solution.py:66
  49.1 4.2 %all-to-all-start = ((bf16[128,16,128]{2,0,1:T(8,128)(2,1)}), bf16[128,16,128]{2,0,1:T(8,128)(2,1)}, u32[]{:S(2)}, u32[]{:S(2)}) async-start(bf16[128,16,128]{2,0,1:T(8,128)(2,1)} %copy_bitcast_fusion.2), calls=%async_computation | async-start | bytes 1048576 | tf_op jit(solution)/shard_map/all_to_all | solution.py:64
  53.4 0.7 fusion.40
  54.1 1.3 copy.35
  55.4 1.3 copy.36
  56.7 1.1 pad_maximum_fusion
  57.8 2.1 pad_maximum_fusion.1
  59.9 9.5 %all-to-all-done = bf16[128,16,128]{2,0,1:T(8,128)(2,1)} async-done(((bf16[128,16,128]{2,0,1:T(8,128)(2,1)}), bf16[128,16,128]{2,0,1:T(8,128)(2,1)}, u32[]{:S(2)}, u32[]{:S(2)}) %all-to-all-start) | async-done | bytes 524320 | tf_op jit(solution)/shard_map/all_to_all | solution.py:64
  69.5 59.3 %while.13 = (s32[]{:T(128)}, bf16[4,512,128]{2,1,0:T(8,128)(2,1)}, s32[4]{0:T(128)S(1)}, s32[2048]{0:T(1024)S(1)}, bf16[2048,128]{1,0:T(8,128)(2,1)}, /*index=5*...) while((s32[]{:T(128)}, bf16[4,512,128]{2,1,0:T(8,128)(2,1)}, ...), condition=%wide.region_5.6_spmd.clone, body=%wide.region_2.5_spmd.clone.sunk | while | flops 1095930880 | bytes 35980072 | solution.py:100
  69.5 0.7 dynamic_slice.31
  70.9 4.4 %compare_select_fusion.8 = s32[2048,1]{0,1:T(1,128)S(1)} fusion(s32[]{:T(128)} %get-tuple-element.364, s32[]{:T(128)} %get-tuple-element.365, s32[]{:T(128)} %get-tuple-element.366, s32[]{:T(128)} %get-tuple-element.367, s32[]{:T(128)} %get-tuple-element.368, s32[]{:T(128)} %get-tuple-element.369, s32[]{:T(128)} %get-tuple-element.370), kind=kLoop, calls=%fused_computation.19.clone.1 | loop fusion | flops 47104 | bytes 8220 | tf_op jit(solution)/shard_map/gather | solution.py:78
  75.9 1.4 broadcast_compare_fusion.2
  77.4 2.8 %fusion.58 = (f32[512]{0:T(512)S(1)}, f32[512,4096]{1,0:T(8,128)S(1)}) fusion(bf16[4096,128]{1,0:T(8,128)(2,1)S(1)} %get-tuple-element.362, bf16[2048,128]{1,0:T(8,128)(2,1)} %get-tuple-element.361, s32[]{:T(128)S(6)} %select_n.210, pred[512,2048]{1,0:T(32,128)(4,1)S(1)} %get-tuple-element.315, pred[512,2048]{1,0:T(32,128)(4,1)S(1)} %get-tuple-element.316), kind=kOutput, calls=%fused_computation.82.clone.1 | convolution fusion | flops 545259008 | bytes 11667460 | tf_op jit(solution)/shard_map/while/body/eval_jaxpr/qhd,khd->hqk/dot_general | solution.py:34
  80.2 1.3 fusion.59
  81.5 2.8 %fusion.60 = bf16[4,512,128]{2,1,0:T(8,128)(2,1)} fusion(bf16[4,512,128]{2,1,0:T(8,128)(2,1)} %get-tuple-element.339, s32[]{:T(128)} %get-tuple-element.338, bf16[4096,128]{1,0:T(8,128)(2,1)S(1)} %copy-done.2, f32[512,4096]{1,0:T(8,128)S(1)} %get-tuple-element.317, f32[512]{0:T(512)S(1)} %fusion.59, f32[512]{0:T(512)S(1)} %get-tuple-element.318), kind=kOutput, calls=%fused_computation.11.clone.1 | convolution fusion | flops 543227904 | bytes 9572864 | tf_op jit(solution)/shard_map/while/body/eval_jaxpr/hqk,khd->qhd/dot_general | solution.py:41
  84.3 0.7 dynamic_slice.31
  85.7 4.4 %compare_select_fusion.8 = s32[2048,1]{0,1:T(1,128)S(1)} fusion(s32[]{:T(128)} %get-tuple-element.364, s32[]{:T(128)} %get-tuple-element.365, s32[]{:T(128)} %get-tuple-element.366, s32[]{:T(128)} %get-tuple-element.367, s32[]{:T(128)} %get-tuple-element.368, s32[]{:T(128)} %get-tuple-element.369, s32[]{:T(128)} %get-tuple-element.370), kind=kLoop, calls=%fused_computation.19.clone.1 | loop fusion | flops 47104 | bytes 8220 | tf_op jit(solution)/shard_map/gather | solution.py:78
  90.7 1.4 broadcast_compare_fusion.2
  92.2 2.8 %fusion.58 = (f32[512]{0:T(512)S(1)}, f32[512,4096]{1,0:T(8,128)S(1)}) fusion(bf16[4096,128]{1,0:T(8,128)(2,1)S(1)} %get-tuple-element.362, bf16[2048,128]{1,0:T(8,128)(2,1)} %get-tuple-element.361, s32[]{:T(128)S(6)} %select_n.210, pred[512,2048]{1,0:T(32,128)(4,1)S(1)} %get-tuple-element.315, pred[512,2048]{1,0:T(32,128)(4,1)S(1)} %get-tuple-element.316), kind=kOutput, calls=%fused_computation.82.clone.1 | convolution fusion | flops 545259008 | bytes 11667460 | tf_op jit(solution)/shard_map/while/body/eval_jaxpr/qhd,khd->hqk/dot_general | solution.py:34
  95.0 1.3 fusion.59
  96.3 2.8 %fusion.60 = bf16[4,512,128]{2,1,0:T(8,128)(2,1)} fusion(bf16[4,512,128]{2,1,0:T(8,128)(2,1)} %get-tuple-element.339, s32[]{:T(128)} %get-tuple-element.338, bf16[4096,128]{1,0:T(8,128)(2,1)S(1)} %copy-done.2, f32[512,4096]{1,0:T(8,128)S(1)} %get-tuple-element.317, f32[512]{0:T(512)S(1)} %fusion.59, f32[512]{0:T(512)S(1)} %get-tuple-element.318), kind=kOutput, calls=%fused_computation.11.clone.1 | convolution fusion | flops 543227904 | bytes 9572864 | tf_op jit(solution)/shard_map/while/body/eval_jaxpr/hqk,khd->qhd/dot_general | solution.py:41
  99.1 0.7 dynamic_slice.31
  100.5 4.4 %compare_select_fusion.8 = s32[2048,1]{0,1:T(1,128)S(1)} fusion(s32[]{:T(128)} %get-tuple-element.364, s32[]{:T(128)} %get-tuple-element.365, s32[]{:T(128)} %get-tuple-element.366, s32[]{:T(128)} %get-tuple-element.367, s32[]{:T(128)} %get-tuple-element.368, s32[]{:T(128)} %get-tuple-element.369, s32[]{:T(128)} %get-tuple-element.370), kind=kLoop, calls=%fused_computation.19.clone.1 | loop fusion | flops 47104 | bytes 8220 | tf_op jit(solution)/shard_map/gather | solution.py:78
  105.5 1.4 broadcast_compare_fusion.2
  107.0 2.8 %fusion.58 = (f32[512]{0:T(512)S(1)}, f32[512,4096]{1,0:T(8,128)S(1)}) fusion(bf16[4096,128]{1,0:T(8,128)(2,1)S(1)} %get-tuple-element.362, bf16[2048,128]{1,0:T(8,128)(2,1)} %get-tuple-element.361, s32[]{:T(128)S(6)} %select_n.210, pred[512,2048]{1,0:T(32,128)(4,1)S(1)} %get-tuple-element.315, pred[512,2048]{1,0:T(32,128)(4,1)S(1)} %get-tuple-element.316), kind=kOutput, calls=%fused_computation.82.clone.1 | convolution fusion | flops 545259008 | bytes 11667460 | tf_op jit(solution)/shard_map/while/body/eval_jaxpr/qhd,khd->hqk/dot_general | solution.py:34
  109.8 1.3 fusion.59
  111.1 2.8 %fusion.60 = bf16[4,512,128]{2,1,0:T(8,128)(2,1)} fusion(bf16[4,512,128]{2,1,0:T(8,128)(2,1)} %get-tuple-element.339, s32[]{:T(128)} %get-tuple-element.338, bf16[4096,128]{1,0:T(8,128)(2,1)S(1)} %copy-done.2, f32[512,4096]{1,0:T(8,128)S(1)} %get-tuple-element.317, f32[512]{0:T(512)S(1)} %fusion.59, f32[512]{0:T(512)S(1)} %get-tuple-element.318), kind=kOutput, calls=%fused_computation.11.clone.1 | convolution fusion | flops 543227904 | bytes 9572864 | tf_op jit(solution)/shard_map/while/body/eval_jaxpr/hqk,khd->qhd/dot_general | solution.py:41
  113.9 0.7 dynamic_slice.31
  115.4 4.4 %compare_select_fusion.8 = s32[2048,1]{0,1:T(1,128)S(1)} fusion(s32[]{:T(128)} %get-tuple-element.364, s32[]{:T(128)} %get-tuple-element.365, s32[]{:T(128)} %get-tuple-element.366, s32[]{:T(128)} %get-tuple-element.367, s32[]{:T(128)} %get-tuple-element.368, s32[]{:T(128)} %get-tuple-element.369, s32[]{:T(128)} %get-tuple-element.370), kind=kLoop, calls=%fused_computation.19.clone.1 | loop fusion | flops 47104 | bytes 8220 | tf_op jit(solution)/shard_map/gather | solution.py:78
  120.4 1.4 broadcast_compare_fusion.2
  121.8 2.8 %fusion.58 = (f32[512]{0:T(512)S(1)}, f32[512,4096]{1,0:T(8,128)S(1)}) fusion(bf16[4096,128]{1,0:T(8,128)(2,1)S(1)} %get-tuple-element.362, bf16[2048,128]{1,0:T(8,128)(2,1)} %get-tuple-element.361, s32[]{:T(128)S(6)} %select_n.210, pred[512,2048]{1,0:T(32,128)(4,1)S(1)} %get-tuple-element.315, pred[512,2048]{1,0:T(32,128)(4,1)S(1)} %get-tuple-element.316), kind=kOutput, calls=%fused_computation.82.clone.1 | convolution fusion | flops 545259008 | bytes 11667460 | tf_op jit(solution)/shard_map/while/body/eval_jaxpr/qhd,khd->hqk/dot_general | solution.py:34
  124.6 1.3 fusion.59
  125.9 2.8 %fusion.60 = bf16[4,512,128]{2,1,0:T(8,128)(2,1)} fusion(bf16[4,512,128]{2,1,0:T(8,128)(2,1)} %get-tuple-element.339, s32[]{:T(128)} %get-tuple-element.338, bf16[4096,128]{1,0:T(8,128)(2,1)S(1)} %copy-done.2, f32[512,4096]{1,0:T(8,128)S(1)} %get-tuple-element.317, f32[512]{0:T(512)S(1)} %fusion.59, f32[512]{0:T(512)S(1)} %get-tuple-element.318), kind=kOutput, calls=%fused_computation.11.clone.1 | convolution fusion | flops 543227904 | bytes 9572864 | tf_op jit(solution)/shard_map/while/body/eval_jaxpr/hqk,khd->qhd/dot_general | solution.py:41
  128.7 4.3 %all-to-all-start.3 = ((bf16[16,128,128]{2,1,0:T(8,128)(2,1)}), bf16[16,128,128]{2,1,0:T(8,128)(2,1)S(1)}, u32[]{:S(2)}, u32[]{:S(2)}) async-start(bf16[16,128,128]{2,1,0:T(8,128)(2,1)} %bitcast.18), calls=%async_computation.3 | async-start | bytes 1048576 | tf_op jit(solution)/shard_map/all_to_all | solution.py:107
  133.1 1.3 dynamic-slice
  134.9 2.4 fusion.33
  137.3 11.9 %all-to-all-done.3 = bf16[16,128,128]{2,1,0:T(8,128)(2,1)S(1)} async-done(((bf16[16,128,128]{2,1,0:T(8,128)(2,1)}), bf16[16,128,128]{2,1,0:T(8,128)(2,1)S(1)}, u32[]{:S(2)}, u32[]{:S(2)}) %all-to-all-start.3) | async-done | bytes 524320 | tf_op jit(solution)/shard_map/all_to_all | solution.py:107
  149.4 2.5 %fusion.20 = f32[128]{0:T(128)S(1)} fusion(bf16[2048,64]{0,1:T(8,128)(2,1)S(1)} %copy-done.6, f32[128,4096]{1,0:T(8,128)} %fusion.33, f32[128]{0:T(128)S(1)} %get-tuple-element.211, f32[128]{0:T(128)S(1)} %get-tuple-element.210, f32[128,64]{0,1:T(8,128)S(1)} %copy-done.7, f32[128,64]{0,1:T(8,128)S(1)} %copy-done.8, bf16[16,128,128]{2,1,0:T(8,128)(2,1)S(1)} %all-to-all-done.3), kind=kOutput, calls=%fused_computation.43 | convolution fusion | flops 202932096 | bytes 2950656 | tf_op jit(solution)/shard_map/dot_general | solution.py:114
  152.8 25.0 %psum.7 = f32[8]{0:T(128)S(1)} all-reduce(f32[8]{0:T(128)S(1)} %select_reduce_fusion.1), channel_id=1, replica_groups=mesh['dp'=32,'seq'=16] {'seq'}, use_global_device_ids=true, to_apply=%region_10.11 | all-reduce | flops 8 | bytes 64 | tf_op jit(solution)/shard_map/psum | solution.py:121
  177.9 71.7 %all-reduce = f32[256]{0:T(256)S(1)} all-reduce(f32[256]{0:T(256)S(1)} %divide_dynamic-update-slice_fusion), channel_id=1, replica_groups=mesh['dp'=32,'seq'=16] {'dp'}, use_global_device_ids=true, to_apply=%add | all-reduce | flops 256 | bytes 2048
  249.6 0.7 select_reduce_fusion
  (57 shorter events, 4.1 us)
Async XLA Ops:
  0.0 134.5 %copy-start = (bf16[256,4096]{1,0:T(8,128)(2,1)S(1)}, bf16[256,4096]{1,0:T(8,128)(2,1)}, u32[]{:S(2)}) copy-start(bf16[256,4096]{1,0:T(8,128)(2,1)} %param.21) | copy-start | bytes 6291460
  0.0 32.9 %copy-start.4 = (s32[1,8]{1,0:T(1,128)S(1)}, s32[1,8]{1,0:T(1,128)}, u32[]{:S(2)}) copy-start(s32[1,8]{1,0:T(1,128)} %param.19) | copy-start | bytes 100
  0.0 35.2 %copy-start.1 = (bf16[8,256,2,128]{3,2,1,0:T(2,128)(2,1)S(1)}, bf16[8,256,2,128]{3,2,1,0:T(2,128)(2,1)}, u32[]{:S(2)}) copy-start(bf16[8,256,2,128]{3,2,1,0:T(2,128)(2,1)} %param.17) | copy-start | bytes 3145732
  2.1 26.6 %all-to-all-start.1 = ((bf16[128,16,128]{2,0,1:T(8,128)(2,1)}), bf16[128,16,128]{2,0,1:T(8,128)(2,1)}, u32[]{:S(2)}, u32[]{:S(2)}) async-start(bf16[128,16,128]{2,0,1:T(8,128)(2,1)} %copy_bitcast_fusion.1), calls=%async_computation.1 | async-start | bytes 1048576 | tf_op jit(solution)/shard_map/all_to_all | solution.py:65
  12.6 40.8 %copy-start.3 = (s32[8]{0:T(128)S(1)}, s32[8]{0:T(128)}, u32[]{:S(2)}) copy-start(s32[8]{0:T(128)} %param.18) | copy-start | bytes 100
  28.7 20.5 %all-to-all-start.2 = ((bf16[128,16,128]{2,0,1:T(8,128)(2,1)}), bf16[128,16,128]{2,0,1:T(8,128)(2,1)}, u32[]{:S(2)}, u32[]{:S(2)}) async-start(bf16[128,16,128]{2,0,1:T(8,128)(2,1)} %copy_bitcast_fusion), calls=%async_computation.2 | async-start | bytes 1048576 | tf_op jit(solution)/shard_map/all_to_all | solution.py:66
  49.1 20.3 %all-to-all-start = ((bf16[128,16,128]{2,0,1:T(8,128)(2,1)}), bf16[128,16,128]{2,0,1:T(8,128)(2,1)}, u32[]{:S(2)}, u32[]{:S(2)}) async-start(bf16[128,16,128]{2,0,1:T(8,128)(2,1)} %copy_bitcast_fusion.2), calls=%async_computation | async-start | bytes 1048576 | tf_op jit(solution)/shard_map/all_to_all | solution.py:64
  69.5 63.6 %copy-start.9 = (s32[8]{0:T(128)S(1)}, s32[8]{0:T(128)}, u32[]{:S(2)}) copy-start(s32[8]{0:T(128)} %param.20) | copy-start | bytes 100
  80.2 1.3 copy-start.2
  95.0 1.3 copy-start.2
  109.8 1.3 copy-start.2
  124.6 1.3 copy-start.2
  128.7 20.7 %copy-start.6 = (bf16[2048,64]{0,1:T(8,128)(2,1)S(1)}, bf16[2048,64]{0,1:T(8,128)(2,1)}, u32[]{:S(2)}) copy-start(bf16[2048,64]{0,1:T(8,128)(2,1)} %param.22) | copy-start | bytes 786436
  128.7 20.7 %copy-start.7 = (f32[128,64]{0,1:T(8,128)S(1)}, f32[128,64]{0,1:T(8,128)}, u32[]{:S(2)}) copy-start(f32[128,64]{0,1:T(8,128)} %param.23) | copy-start | bytes 98308
  128.7 20.7 %copy-start.8 = (f32[128,64]{0,1:T(8,128)S(1)}, f32[128,64]{0,1:T(8,128)}, u32[]{:S(2)}) copy-start(f32[128,64]{0,1:T(8,128)} %param.24) | copy-start | bytes 98308
  128.7 120.9 %copy-start.5 = (s32[8]{0:T(128)S(1)}, s32[8]{0:T(128)}, u32[]{:S(2)}) copy-start(s32[8]{0:T(128)} %param.25) | copy-start | bytes 100
  128.7 20.4 %all-to-all-start.3 = ((bf16[16,128,128]{2,1,0:T(8,128)(2,1)}), bf16[16,128,128]{2,1,0:T(8,128)(2,1)S(1)}, u32[]{:S(2)}, u32[]{:S(2)}) async-start(bf16[16,128,128]{2,1,0:T(8,128)(2,1)} %bitcast.18), calls=%async_computation.3 | async-start | bytes 1048576 | tf_op jit(solution)/shard_map/all_to_all | solution.py:107
where the time goes:
time: 252 us; the launch traced here: 250 us
  blocking collectives  96.8 us (38%)
  waiting for transfers between devices  47 us (19%)
  other arithmetic  35.6 us (14%)
  matrix products  27.8 us (11%)
  starting transfers between devices  23.2 us (9%)
  local copies, waits for them, and re-layouts  16.2 us (6%)
  loops' own time  3.01 us (1%)
    unnamed x1, blocking collectives  71.7 us
    psum x1, blocking collectives, per_device(): clip_totals = lax.psum(clip_partial, 'seq')  25 us
    gather x8, other arithmetic, per_device(): text_live = text_slots % text_len < text_lengths[text_clip]  17.8 us
    all_to_all x1, waiting for transfers between devices, per_device(): lax.all_to_all(keys, 'seq', split_axis=1, concat_axis=0, tiled=True)  14.1 us
    all_to_all x1, waiting for transfers between devices, per_device(): lax.all_to_all(attended, 'seq', split_axis=0, concat_axis=1, tiled=True)  11.9 us
    all_to_all x1, waiting for transfers between devices, per_device(): lax.all_to_all(values, 'seq', split_axis=1, concat_axis=0, tiled=True)  11.4 us
    dot_general x4, matrix products, attend_block(): jnp.einsum('hqk,khd->qhd', weights, value_split, preferred_element_type=j...  11.3 us
    dot_general x4, matrix products, attend_block(): jnp.einsum('qhd,khd->hqk', query_split, key_split, preferred_element_type...  11.2 us
  transfers between devices with their start and end apart: 4, of which 4 were waited for; matrix products, arithmetic and copies ran while one was open for 7% of the time, Pallas kernels for 0%

commit v1 on v0

v1 whole, which is shorter than its diff:
```python
import functools
import math

import jax
import jax.numpy as jnp
from jax import lax
from jax.experimental import pallas as pl
from jax.experimental.pallas import tpu as pltpu
from jax.sharding import PartitionSpec as P

MESH = pl.DeviceIdType.MESH
HEAD_DIM = 128
FREQ = 256
CLIPS = 8
TEXT = 256
CHANNELS = 64
WIDTH = 2048
TOK = 128
N_SEQ = 16
N_DP = 32
ROWS = TOK * N_SEQ
BLOCK = 256
BLOCKS = ROWS // BLOCK
PAD = 512
WINDOW = BLOCK + 2 * PAD
NEAR_CLIPS = 5
SPAN = NEAR_CLIPS * TEXT
MSG = 80
FAR = 65536.0
EPS = 1e-06
SCALE = math.log2(math.e) / math.sqrt(HEAD_DIM)
NT = (((1,), (1,)), ((), ()))
F32 = jnp.float32
BF16 = jnp.bfloat16


def step_embedding(timesteps):
    half_width = FREQ // 2
    frequency = jnp.exp(-math.log(10000.0) * jnp.arange(half_width, dtype=F32) / half_width)
    angles = timesteps.astype(F32)[:, None] * frequency[None, :]
    return jnp.concatenate([jnp.cos(angles), jnp.sin(angles)], axis=1)


def nt_dot(a, b):
    return lax.dot_general(a, b, NT, preferred_element_type=F32)


def nn_dot(a, b):
    return jnp.dot(a, b, preferred_element_type=F32)


def pieces(x, count):
    out = []
    for _ in range(count):
        piece = x.astype(BF16)
        out.append(piece)
        x = x - piece.astype(F32)
    return out


def along(scalars, shape, dim):
    place = lax.broadcasted_iota(jnp.int32, shape, dim)
    out = jnp.zeros(shape, jnp.int32)
    for index, scalar in enumerate(scalars):
        out = jnp.where(place == index, scalar, out)
    return out


PARTNERS = [(4, 1), (4, 0), (3, 0), (-3, 0), (3, 1), (-3, 1), (2, 0), (-2, 0), (2, 1), (-2, 1)]
PARTNERS += [(1, 0), (-1, 0), (1, 1), (-1, 1), (0, 1)]


def kernel(
    q_hbm, k_hbm, v_hbm, text_hbm, act_ref, tlen_ref, clen_ref, order_ref, modw_hbm, finw_hbm, noise_hbm, clean_hbm,
    out_ref,
    qbuf, kbuf, vbuf, textbuf, modw, finw, noise, clean,
    tk, tv, qbias, kbias, tbias, onehot, clip_row, wall, btok, ctok, target,
    text_max, text_sum, text_out, inverse, weights, message, gathered, part_out, part_in, loss_out, loss_in,
    in_send, in_recv, own_sem, load_sem, msg_send, msg_recv, part_send, part_recv, loss_send, loss_recv,
):
    me = lax.axis_index("seq")
    dp = lax.axis_index("dp")
    z = me // 2
    core = me % 2
    peers = [lax.rem(z + dz + 8, 8) * 2 + lax.rem(core + dc, 2) for dz, dc in PARTNERS]

    loads = [
        pltpu.make_async_copy(src, dst, load_sem.at[i])
        for i, (src, dst) in enumerate(
            [(text_hbm, textbuf), (modw_hbm, modw), (finw_hbm, finw), (noise_hbm, noise), (clean_hbm, clean)]
        )
    ]
    for load in loads:
        load.start()
    own = []
    for t, (src, dst, base) in enumerate([(q_hbm, qbuf, 0), (k_hbm, kbuf, PAD), (v_hbm, vbuf, PAD)]):
        own.append(
            pltpu.make_async_copy(
                src.at[:, pl.ds(pl.multiple_of(me * HEAD_DIM, HEAD_DIM), HEAD_DIM)],
                dst.at[pl.ds(pl.multiple_of(base + me * TOK, TOK), TOK)],
                own_sem.at[t],
            )
        )
        own[-1].start()

    barrier = pltpu.get_barrier_semaphore()
    for peer in peers:
        pl.semaphore_signal(barrier, inc=1, device_id=(dp, peer), device_id_type=MESH)
    for i in range(1, N_DP):
        pl.semaphore_signal(barrier, inc=1, device_id=(lax.rem(dp + i, N_DP), me), device_id_type=MESH)
    pl.semaphore_wait(barrier, N_SEQ - 1 + N_DP - 1)

    sends = []
    for t, (src, dst, base) in enumerate([(q_hbm, qbuf, 0), (k_hbm, kbuf, PAD), (v_hbm, vbuf, PAD)]):
        row = []
        for j, peer in enumerate(peers):
            copy = pltpu.make_async_remote_copy(
                src_ref=src.at[:, pl.ds(pl.multiple_of(peer * HEAD_DIM, HEAD_DIM), HEAD_DIM)],
                dst_ref=dst.at[pl.ds(pl.multiple_of(base + me * TOK, TOK), TOK)],
                send_sem=in_send.at[t, j],
                recv_sem=in_recv.at[t, j],
                device_id=(dp, peer),
                device_id_type=MESH,
            )
            copy.start()
            row.append(copy)
        sends.append(row)

    starts, ends = [], []
    total = jnp.int32(0)
    for c in range(CLIPS):
        starts.append(total)
        total = total + clen_ref[0, c]
        ends.append(total)
    start_lane, end_lane = along(starts, (1, HEAD_DIM), 1), along(ends, (1, HEAD_DIM), 1)
    start_col, end_col = along(starts, (CLIPS, 1), 0), along(ends, (CLIPS, 1), 0)
    size_col = (end_col - start_col).astype(F32)
    place = lax.broadcasted_iota(jnp.int32, (CLIPS, ROWS), 1)
    onehot[...] = jnp.where((place >= start_col) & (place < end_col), 1.0, 0.0)
    clip_of = jnp.zeros((CLIPS, ROWS), jnp.int32)
    for c in range(1, CLIPS):
        clip_of = clip_of + jnp.where(place >= starts[c], 1, 0)
    clip_row[...] = clip_of
    edge = jnp.zeros((PAD, HEAD_DIM), BF16)
    for buf in (kbuf, vbuf):
        buf[pl.ds(0, PAD), :] = edge
        buf[pl.ds(PAD + ROWS, PAD), :] = edge

    rows_iota = lax.broadcasted_iota(jnp.int32, (BLOCK, HEAD_DIM), 0)
    lane_iota = lax.broadcasted_iota(jnp.int32, (BLOCK, HEAD_DIM), 1)

    def fill_key_bias(i, _):
        token = rows_iota + (i * BLOCK - PAD)
        live = (token >= start_lane) & (token < end_lane)
        kbias[pl.ds(pl.multiple_of(i * BLOCK, BLOCK), BLOCK), :] = jnp.where(live, 0.0, -FAR).astype(BF16)
        return 0

    def fill_query_bias(i, _):
        token = rows_iota + i * BLOCK
        live = (token >= start_lane) & (token < end_lane)
        qbias[pl.ds(pl.multiple_of(i * BLOCK, BLOCK), BLOCK), :] = jnp.where(live, 1.0, 0.0).astype(BF16)
        return 0

    lax.fori_loop(0, (ROWS + 2 * PAD) // BLOCK, fill_key_bias, 0)
    lax.fori_loop(0, BLOCKS, fill_query_bias, 0)

    loads[0].wait()
    sub = lax.broadcasted_iota(jnp.int32, (TEXT, 2 * TEXT), 0)
    lane = lax.broadcasted_iota(jnp.int32, (TEXT, 2 * TEXT), 1)
    pick_key = jnp.where(lane == 2 * sub, 1.0, 0.0).astype(BF16)
    pick_value = jnp.where(lane == 2 * sub + 1, 1.0, 0.0).astype(BF16)
    length_lane = along([tlen_ref[c] for c in range(CLIPS)], (1, HEAD_DIM), 1)

    def split_text(c, _):
        both = textbuf[c]
        rows = pl.ds(pl.multiple_of(c * TEXT, TEXT), TEXT)
        tk[rows, :] = nn_dot(pick_key, both).astype(BF16)
        tv[rows, :] = nn_dot(pick_value, both).astype(BF16)
        live = (lane_iota == c) & (rows_iota < length_lane)
        tbias[rows, :] = jnp.where(live, 0.0, -FAR).astype(BF16)
        return 0

    lax.fori_loop(0, CLIPS, split_text, 0)

    loads[1].wait()
    loads[2].wait()
    act = act_ref[...]
    head_at = pl.multiple_of(me * HEAD_DIM, HEAD_DIM)
    gain = 1.0 + nn_dot(act, modw[:, pl.ds(WIDTH + head_at, HEAD_DIM)])
    turned = finw[:, pl.ds(head_at, HEAD_DIM)].astype(F32)
    for c in range(CLIPS):
        high, low = pieces(turned * gain[c : c + 1, :], 2)
        wall[pl.ds(c * CHANNELS, CHANNELS), :] = jnp.concatenate([high, low], axis=1)
    shift_all = nn_dot(act, modw[:, pl.ds(0, WIDTH)])
    gain_all = 1.0 + nn_dot(act, modw[:, pl.ds(WIDTH, WIDTH)])
    stacked = jnp.concatenate(pieces(gain_all, 3) + pieces(shift_all, 3), axis=0)
    folded = nt_dot(finw[...], stacked)
    gain_sum = folded[:, 0:8] + folded[:, 8:16] + folded[:, 16:24]
    shift_sum = folded[:, 24:32] + folded[:, 32:40] + folded[:, 40:48]
    mine = onehot[:, pl.ds(pl.multiple_of(me * TOK, TOK), TOK)]
    gain_tok = jnp.zeros((CHANNELS, TOK), F32)
    shift_tok = jnp.zeros((CHANNELS, TOK), F32)
    for c in range(CLIPS):
        gain_tok = gain_tok + gain_sum[:, c : c + 1] * mine[c : c + 1, :]
        shift_tok = shift_tok + shift_sum[:, c : c + 1] * mine[c : c + 1, :]
    btok[...] = gain_tok
    ctok[...] = shift_tok
    loads[3].wait()
    loads[4].wait()
    target[...] = noise[...] - clean[...]
    order_lane = along([order_ref[c] for c in range(CLIPS)], (1, HEAD_DIM), 1)

    own[0].wait()
    for copy in sends[0]:
        copy.wait_recv()
    one_lanes = jnp.ones((SPAN, HEAD_DIM), BF16)

    def text_block(b, _):
        rows = pl.ds(pl.multiple_of(b * BLOCK, BLOCK), BLOCK)
        span = pl.ds(pl.multiple_of(b // 2 * TEXT, TEXT), SPAN)
        left = jnp.concatenate([qbuf[rows, :], qbias[rows, :]], axis=1)
        right = jnp.concatenate([tk[span, :], tbias[span, :]], axis=1)
        scores = nt_dot(left, right)
        top = jnp.max(scores, axis=1, keepdims=True)
        weight = jnp.exp2((scores - top) * SCALE).astype(BF16)
        mixed = nn_dot(weight, jnp.concatenate([tv[span, :], one_lanes], axis=1))
        text_max[rows, :] = jnp.broadcast_to(top, (BLOCK, HEAD_DIM))
        text_out[rows, :] = mixed[:, :HEAD_DIM]
        text_sum[rows, :] = mixed[:, HEAD_DIM:]
        return 0

    lax.fori_loop(0, BLOCKS, text_block, 0)

    own[1].wait()
    for copy in sends[1]:
        copy.wait_recv()
    one_wide = jnp.ones((WINDOW, HEAD_DIM), BF16)

    def score_block(b, _):
        rows = pl.ds(pl.multiple_of(b * BLOCK, BLOCK), BLOCK)
        window = pl.ds(pl.multiple_of(b * BLOCK, BLOCK), WINDOW)
        left = jnp.concatenate([qbuf[rows, :], qbias[rows, :]], axis=1)
        right = jnp.concatenate([kbuf[window, :], kbias[window, :]], axis=1)
        scores = nt_dot(left, right)
        before = text_max[rows, :]
        top = jnp.maximum(before, jnp.max(scores, axis=1, keepdims=True))
        weight = jnp.exp2((scores - top[:, :1]) * SCALE).astype(BF16)
        weights[rows, :] = weight
        fade = jnp.exp2((before - top) * SCALE)
        inv = 1.0 / (nn_dot(weight, one_wide) + text_sum[rows, :] * fade)
        inverse[rows, :] = inv
        text_out[rows, :] = text_out[rows, :] * (fade * inv)
        return 0

    lax.fori_loop(0, BLOCKS, score_block, 0)

    own[2].wait()
    for copy in sends[2]:
        copy.wait_recv()
    ones_row = jnp.ones((8, 2 * HEAD_DIM), BF16)
    row8 = lax.broadcasted_iota(jnp.int32, (8, TOK), 0)

    def message_copy(owner):
        return pltpu.make_async_remote_copy(
            src_ref=message.at[owner],
            dst_ref=gathered.at[me],
            send_sem=msg_send.at[owner],
            recv_sem=msg_recv.at[me],
            device_id=(dp, owner),
            device_id_type=MESH,
        )

    def value_block(i, _):
        reach = (i + 1) // 2
        step = 4 + reach - 2 * reach * lax.rem(i, 2)
        b = lax.rem(z + step, 8)
        rows = pl.ds(pl.multiple_of(b * BLOCK, BLOCK), BLOCK)
        window = pl.ds(pl.multiple_of(b * BLOCK, BLOCK), WINDOW)
        first = b // 2
        mixed = nn_dot(weights[rows, :], vbuf[window, :])
        attended = (mixed * inverse[rows, :] + text_out[rows, :]).astype(BF16)
        fold = wall[pl.ds(pl.multiple_of(first * CHANNELS, CHANNELS), NEAR_CLIPS * CHANNELS), :]
        for half in range(2):
            owner = 2 * b + half
            part = attended[half * TOK : (half + 1) * TOK]
            spread = nt_dot(fold, jnp.concatenate([part, part], axis=1))
            picked = jnp.zeros((CHANNELS, TOK), F32)
            clip_here = clip_row[0:1, pl.ds(pl.multiple_of(owner * TOK, TOK), TOK)]
            for j in range(NEAR_CLIPS):
                picked = jnp.where(clip_here == first + j, spread[j * CHANNELS : (j + 1) * CHANNELS], picked)
            wide_part = part.astype(F32)
            total = nt_dot(ones_row[:, :HEAD_DIM], part)
            squares = nt_dot(ones_row, jnp.concatenate(pieces(wide_part * wide_part, 2), axis=1))
            total_high, total_low = [x.astype(F32) for x in pieces(total, 2)]
            square_high, square_low = [x.astype(F32) for x in pieces(squares, 2)]
            stats = jnp.where(row8 == 0, total_high, jnp.where(row8 == 1, total_low, jnp.where(row8 == 2, square_high, square_low)))
            message[owner] = jnp.concatenate([picked, stats, jnp.zeros((8, TOK), F32)], axis=0).astype(BF16)

            @pl.when(owner != me)
            def _():
                message_copy(owner).start()

        return 0

    lax.fori_loop(0, BLOCKS, value_block, 0)

    total = message[me].astype(F32)
    for peer in peers:
        pltpu.make_async_remote_copy(
            src_ref=message.at[peer],
            dst_ref=gathered.at[peer],
            send_sem=msg_send.at[peer],
            recv_sem=msg_recv.at[peer],
            device_id=(dp, peer),
            device_id_type=MESH,
        ).wait_recv()
        total = total + gathered[peer].astype(F32)
    center = (total[64:65] + total[65:66]) / WIDTH
    spread = (total[66:67] + total[67:68]) / WIDTH - center * center
    predicted = lax.rsqrt(spread + EPS) * (total[:CHANNELS] - center * btok[...]) + ctok[...]
    difference = predicted - target[...]
    error = jnp.sum(difference * difference, axis=0, keepdims=True) / CHANNELS
    mine = onehot[:, pl.ds(pl.multiple_of(me * TOK, TOK), TOK)]
    partial = jnp.broadcast_to(jnp.sum(mine * error, axis=1, keepdims=True), (CLIPS, HEAD_DIM))
    part_out[...] = partial
    parts = []
    for j, peer in enumerate(peers):
        copy = pltpu.make_async_remote_copy(
            src_ref=part_out,
            dst_ref=part_in.at[j],
            send_sem=part_send.at[j],
            recv_sem=part_recv.at[j],
            device_id=(dp, peer),
            device_id_type=MESH,
        )
        copy.start()
        parts.append(copy)
    for j, copy in enumerate(parts):
        copy.wait_recv()
        partial = partial + part_in[j]
    losses = partial / size_col
    loss_out[...] = losses
    lefts = []
    for i in range(1, N_DP):
        copy = pltpu.make_async_remote_copy(
            src_ref=loss_out,
            dst_ref=loss_in.at[i],
            send_sem=loss_send.at[i],
            recv_sem=loss_recv.at[i],
            device_id=(lax.rem(dp + i, N_DP), me),
            device_id_type=MESH,
        )
        copy.start()
        lefts.append(copy)
    slot = lax.broadcasted_iota(jnp.int32, (CLIPS, HEAD_DIM), 0)
    scores = jnp.where(slot + dp * CLIPS == order_lane, losses, 0.0)
    for i in range(1, N_DP):
        lefts[i - 1].wait_recv()
        group = lax.rem(dp - i + N_DP, N_DP)
        scores = scores + jnp.where(slot + group * CLIPS == order_lane, loss_in[i], 0.0)
    out_ref[...] = jnp.sum(scores, axis=0, keepdims=True)

    for row in sends:
        for copy in row:
            copy.wait_send()
    for peer in peers:
        message_copy(peer).wait_send()
    for copy in parts:
        copy.wait_send()
    for copy in lefts:
        copy.wait_send()


def per_device(
    queries, keys, values, text_kv, text_lengths, clip_lengths, timesteps, mod_weight, final_weight, noise, clean, report_order
):
    activated = jax.nn.silu(step_embedding(timesteps)).astype(BF16)
    text = text_kv.reshape(CLIPS, 2 * TEXT, HEAD_DIM)
    anywhere = pl.BlockSpec(memory_space=pl.ANY)
    vmem = pl.BlockSpec(memory_space=pltpu.VMEM)
    smem = pl.BlockSpec(memory_space=pltpu.SMEM)
    dma = pltpu.SemaphoreType.DMA
    out = pl.pallas_call(
        kernel,
        out_shape=jax.ShapeDtypeStruct((1, HEAD_DIM), F32),
        in_specs=[anywhere] * 4 + [vmem] + [smem] * 3 + [anywhere] * 4,
        out_specs=vmem,
        scratch_shapes=[
            pltpu.VMEM((ROWS, HEAD_DIM), BF16),
            pltpu.VMEM((ROWS + 2 * PAD, HEAD_DIM), BF16),
            pltpu.VMEM((ROWS + 2 * PAD, HEAD_DIM), BF16),
            pltpu.VMEM((CLIPS, 2 * TEXT, HEAD_DIM), BF16),
            pltpu.VMEM((FREQ, 2 * WIDTH), BF16),
            pltpu.VMEM((CHANNELS, WIDTH), BF16),
            pltpu.VMEM((CHANNELS, TOK), F32),
            pltpu.VMEM((CHANNELS, TOK), F32),
            pltpu.VMEM((CLIPS * TEXT, HEAD_DIM), BF16),
            pltpu.VMEM((CLIPS * TEXT, HEAD_DIM), BF16),
            pltpu.VMEM((ROWS, HEAD_DIM), BF16),
            pltpu.VMEM((ROWS + 2 * PAD, HEAD_DIM), BF16),
            pltpu.VMEM((CLIPS * TEXT, HEAD_DIM), BF16),
            pltpu.VMEM((CLIPS, ROWS), F32),
            pltpu.VMEM((CLIPS, ROWS), jnp.int32),
            pltpu.VMEM((CLIPS * CHANNELS, 2 * HEAD_DIM), BF16),
            pltpu.VMEM((CHANNELS, TOK), F32),
            pltpu.VMEM((CHANNELS, TOK), F32),
            pltpu.VMEM((CHANNELS, TOK), F32),
            pltpu.VMEM((ROWS, HEAD_DIM), F32),
            pltpu.VMEM((ROWS, HEAD_DIM), F32),
            pltpu.VMEM((ROWS, HEAD_DIM), F32),
            pltpu.VMEM((ROWS, HEAD_DIM), F32),
            pltpu.VMEM((ROWS, WINDOW), BF16),
            pltpu.VMEM((N_SEQ, MSG, TOK), BF16),
            pltpu.VMEM((N_SEQ, MSG, TOK), BF16),
            pltpu.VMEM((CLIPS, HEAD_DIM), F32),
            pltpu.VMEM((N_SEQ, CLIPS, HEAD_DIM), F32),
            pltpu.VMEM((CLIPS, HEAD_DIM), F32),
            pltpu.VMEM((N_DP, CLIPS, HEAD_DIM), F32),
            dma((3, N_SEQ)),
            dma((3, N_SEQ)),
            dma((3,)),
            dma((5,)),
            dma((N_SEQ,)),
            dma((N_SEQ,)),
            dma((N_SEQ,)),
            dma((N_SEQ,)),
            dma((N_DP,)),
            dma((N_DP,)),
        ],
        compiler_params=pltpu.CompilerParams(
            collective_id=0, has_side_effects=True, vmem_limit_bytes=60 * 1024 * 1024
        ),
    )(
        queries, keys, values, text, activated, text_lengths, clip_lengths, report_order, mod_weight, final_weight.T, noise.T, clean.T
    )
    return out[0, :CLIPS]


def solution(mesh):
    rows = P(("dp", "seq"), None)
    in_specs = (
        rows, rows, rows, P("dp", None, None, "seq"), P("dp"), P("dp", None), P("dp"), P(), P(), rows, rows, P("dp"),
    )
    return jax.shard_map(per_device, mesh=mesh, in_specs=in_specs, out_specs=P("dp"), check_vma=False)
```

time: 252 us -> 78.4 us (0.31)
  the two profiles are of different devices: /device:TPU:8 before, /device:TPU:1 now
where the time goes in v1:
time: 78.4 us; the launch traced here: 78.2 us
  Pallas kernels  75.6 us (96%)
  other arithmetic  1.39 us (2%)
  local copies, waits for them, and re-layouts  1.14 us (1%)
    pallas_call x1, Pallas kernels, per_device(): pl.pallas_call(kernel, out_shape=jax.ShapeDtypeStruct((1, HEAD_DIM), F32)...  75.6 us

profile of v1, /device:TPU:1, one launch (start us, length us, event | category | flops | bytes accessed | tf_op | source)
XLA Modules:
  0.0 78.2 jit_solution(15381237542304444869)
XLA Ops:
  0.0 0.7 convert_element_type.6
  0.7 0.1 multiply_cosine_fusion
  0.8 0.6 multiply_convert_fusion.act_ref
  1.4 75.6 %shard_map.118 = f32[1,128]{1,0:T(1,128)} custom-call(bf16[128,2048]{1,0:T(8,128)(2,1)} %q_hbm.1, bf16[128,2048]{1,0:T(8,128)(2,1)} %k_hbm.1, bf16[128,2048]{1,0:T(8,128)(2,1)} %v_hbm.1, bf16[8,512,128]{2,1,0:T(8,128)(2,1)} %bitcast.6, bf16[8,256]{1,0:T(8,128)(2,1)} %multiply_convert_fusion.act_ref, s32[8]{0:T(128)} %tlen_ref.1, s32[1,8]{1,0:T(1,128)} %clen_ref.1, ...), custom_call_target="tpu_custom_call" | custom-call | tf_op jit(solution)/shard_map/pallas_call | solution.py:383
  77.1 1.1 %slice_bitcast_fusion = f32[8]{0:T(128)} fusion(f32[1,128]{1,0:T(1,128)} %shard_map.118), kind=kLoop, calls=%fused_computation.4 | loop fusion | bytes 64 | tf_op jit(solution)/shard_map/squeeze | solution.py:436
  (1 shorter events, 0.0 us)

commit v2 on v1

--- a/solution.py
+++ b/solution.py
@@ -34,13 +34,6 @@
 BF16 = jnp.bfloat16
 
 
-def step_embedding(timesteps):
-    half_width = FREQ // 2
-    frequency = jnp.exp(-math.log(10000.0) * jnp.arange(half_width, dtype=F32) / half_width)
-    angles = timesteps.astype(F32)[:, None] * frequency[None, :]
-    return jnp.concatenate([jnp.cos(angles), jnp.sin(angles)], axis=1)
-
-
 def nt_dot(a, b):
     return lax.dot_general(a, b, NT, preferred_element_type=F32)
 
@@ -66,17 +59,21 @@
     return out
 
 
-PARTNERS = [(4, 1), (4, 0), (3, 0), (-3, 0), (3, 1), (-3, 1), (2, 0), (-2, 0), (2, 1), (-2, 1)]
-PARTNERS += [(1, 0), (-1, 0), (1, 1), (-1, 1), (0, 1)]
+PARTNERS = [(0, 1), (1, 0), (-1, 0), (1, 1), (-1, 1), (2, 0), (-2, 0), (2, 1), (-2, 1)]
+PARTNERS += [(3, 0), (-3, 0), (3, 1), (-3, 1), (4, 0), (4, 1)]
+
+
+def wait_for(buffer, sem):
+    pltpu.make_async_copy(buffer, buffer, sem).wait()
 
 
 def kernel(
-    q_hbm, k_hbm, v_hbm, text_hbm, act_ref, tlen_ref, clen_ref, order_ref, modw_hbm, finw_hbm, noise_hbm, clean_hbm,
+    q_hbm, k_hbm, v_hbm, text_hbm, tlen_hbm, clen_hbm, order_hbm, time_hbm, modw_hbm, finw_hbm, noise_hbm, clean_hbm,
     out_ref,
-    qbuf, kbuf, vbuf, textbuf, modw, finw, noise, clean,
+    qbuf, kbuf, vbuf, textbuf, modw, finw, noise, clean, tlen_ref, clen_ref, order_ref, time_ref,
     tk, tv, qbias, kbias, tbias, onehot, clip_row, wall, btok, ctok, target,
     text_max, text_sum, text_out, inverse, weights, message, gathered, part_out, part_in, loss_out, loss_in,
-    in_send, in_recv, own_sem, load_sem, msg_send, msg_recv, part_send, part_recv, loss_send, loss_recv,
+    load_sem, in_send, in_recv, msg_send, msg_recv, part_send, part_recv, loss_send, loss_recv,
 ):
     me = lax.axis_index("seq")
     dp = lax.axis_index("dp")
@@ -84,47 +81,44 @@
     core = me % 2
     peers = [lax.rem(z + dz + 8, 8) * 2 + lax.rem(core + dc, 2) for dz, dc in PARTNERS]
 
-    loads = [
-        pltpu.make_async_copy(src, dst, load_sem.at[i])
-        for i, (src, dst) in enumerate(
-            [(text_hbm, textbuf), (modw_hbm, modw), (finw_hbm, finw), (noise_hbm, noise), (clean_hbm, clean)]
-        )
-    ]
-    for load in loads:
-        load.start()
-    own = []
-    for t, (src, dst, base) in enumerate([(q_hbm, qbuf, 0), (k_hbm, kbuf, PAD), (v_hbm, vbuf, PAD)]):
-        own.append(
-            pltpu.make_async_copy(
-                src.at[:, pl.ds(pl.multiple_of(me * HEAD_DIM, HEAD_DIM), HEAD_DIM)],
-                dst.at[pl.ds(pl.multiple_of(base + me * TOK, TOK), TOK)],
-                own_sem.at[t],
-            )
-        )
-        own[-1].start()
-
     barrier = pltpu.get_barrier_semaphore()
     for peer in peers:
         pl.semaphore_signal(barrier, inc=1, device_id=(dp, peer), device_id_type=MESH)
     for i in range(1, N_DP):
         pl.semaphore_signal(barrier, inc=1, device_id=(lax.rem(dp + i, N_DP), me), device_id_type=MESH)
+
+    loads = [
+        pltpu.make_async_copy(src, dst, load_sem.at[i])
+        for i, (src, dst) in enumerate(
+            [
+                (tlen_hbm, tlen_ref), (clen_hbm, clen_ref), (order_hbm, order_ref), (time_hbm, time_ref),
+                (text_hbm, textbuf), (modw_hbm, modw), (finw_hbm, finw), (noise_hbm, noise), (clean_hbm, clean),
+            ]
+        )
+    ]
+    for load in loads:
+        load.start()
+    head_at = pl.multiple_of(me * HEAD_DIM, HEAD_DIM)
+    streams = [(q_hbm, qbuf, 0), (k_hbm, kbuf, PAD), (v_hbm, vbuf, PAD)]
+    for t, (src, dst, base) in enumerate(streams):
+        pltpu.make_async_copy(
+            src.at[:, pl.ds(head_at, HEAD_DIM)], dst.at[pl.ds(pl.multiple_of(base + me * TOK, TOK), TOK)], in_recv.at[t]
+        ).start()
+
     pl.semaphore_wait(barrier, N_SEQ - 1 + N_DP - 1)
 
-    sends = []
-    for t, (src, dst, base) in enumerate([(q_hbm, qbuf, 0), (k_hbm, kbuf, PAD), (v_hbm, vbuf, PAD)]):
-        row = []
-        for j, peer in enumerate(peers):
-            copy = pltpu.make_async_remote_copy(
+    for t, (src, dst, base) in enumerate(streams):
+        for peer in reversed(peers):
+            pltpu.make_async_remote_copy(
                 src_ref=src.at[:, pl.ds(pl.multiple_of(peer * HEAD_DIM, HEAD_DIM), HEAD_DIM)],
                 dst_ref=dst.at[pl.ds(pl.multiple_of(base + me * TOK, TOK), TOK)],
-                send_sem=in_send.at[t, j],
-                recv_sem=in_recv.at[t, j],
+                send_sem=in_send.at[t],
+                recv_sem=in_recv.at[t],
                 device_id=(dp, peer),
                 device_id_type=MESH,
-            )
-            copy.start()
-            row.append(copy)
-        sends.append(row)
+            ).start()
+    for load in loads[:4]:
+        load.wait()
 
     starts, ends = [], []
     total = jnp.int32(0)
@@ -134,7 +128,7 @@
         ends.append(total)
     start_lane, end_lane = along(starts, (1, HEAD_DIM), 1), along(ends, (1, HEAD_DIM), 1)
     start_col, end_col = along(starts, (CLIPS, 1), 0), along(ends, (CLIPS, 1), 0)
-    size_col = (end_col - start_col).astype(F32)
+    size_row = jnp.where(end_lane > start_lane, end_lane - start_lane, 1).astype(F32)
     place = lax.broadcasted_iota(jnp.int32, (CLIPS, ROWS), 1)
     onehot[...] = jnp.where((place >= start_col) & (place < end_col), 1.0, 0.0)
     clip_of = jnp.zeros((CLIPS, ROWS), jnp.int32)
@@ -164,7 +158,7 @@
     lax.fori_loop(0, (ROWS + 2 * PAD) // BLOCK, fill_key_bias, 0)
     lax.fori_loop(0, BLOCKS, fill_query_bias, 0)
 
-    loads[0].wait()
+    loads[4].wait()
     sub = lax.broadcasted_iota(jnp.int32, (TEXT, 2 * TEXT), 0)
     lane = lax.broadcasted_iota(jnp.int32, (TEXT, 2 * TEXT), 1)
     pick_key = jnp.where(lane == 2 * sub, 1.0, 0.0).astype(BF16)
@@ -182,10 +176,13 @@
 
     lax.fori_loop(0, CLIPS, split_text, 0)
 
-    loads[1].wait()
-    loads[2].wait()
-    act = act_ref[...]
-    head_at = pl.multiple_of(me * HEAD_DIM, HEAD_DIM)
+    loads[5].wait()
+    loads[6].wait()
+    step = along([time_ref[c] for c in range(CLIPS)], (CLIPS, FREQ // 2), 0).astype(F32)
+    ramp = lax.broadcasted_iota(jnp.int32, (CLIPS, FREQ // 2), 1).astype(F32)
+    angles = step * jnp.exp(-math.log(10000.0) * ramp / (FREQ // 2))
+    embedding = jnp.concatenate([jnp.cos(angles), jnp.sin(angles)], axis=1)
+    act = jax.nn.silu(embedding).astype(BF16)
     gain = 1.0 + nn_dot(act, modw[:, pl.ds(WIDTH + head_at, HEAD_DIM)])
     turned = finw[:, pl.ds(head_at, HEAD_DIM)].astype(F32)
     for c in range(CLIPS):
@@ -205,14 +202,14 @@
         shift_tok = shift_tok + shift_sum[:, c : c + 1] * mine[c : c + 1, :]
     btok[...] = gain_tok
     ctok[...] = shift_tok
-    loads[3].wait()
-    loads[4].wait()
+    loads[7].wait()
+    loads[8].wait()
     target[...] = noise[...] - clean[...]
-    order_lane = along([order_ref[c] for c in range(CLIPS)], (1, HEAD_DIM), 1)
-
-    own[0].wait()
-    for copy in sends[0]:
-        copy.wait_recv()
+    order_col = along([order_ref[c] for c in range(CLIPS)], (CLIPS, HEAD_DIM), 0)
+    order_lane = lax.broadcasted_iota(jnp.int32, (CLIPS, HEAD_DIM), 1)
+    wanted = jnp.where(order_lane < CLIPS, order_col - order_lane, -1)
+
+    wait_for(qbuf, in_recv.at[0])
     one_lanes = jnp.ones((SPAN, HEAD_DIM), BF16)
 
     def text_block(b, _):
@@ -231,9 +228,7 @@
 
     lax.fori_loop(0, BLOCKS, text_block, 0)
 
-    own[1].wait()
-    for copy in sends[1]:
-        copy.wait_recv()
+    wait_for(kbuf.at[pl.ds(PAD, ROWS)], in_recv.at[1])
     one_wide = jnp.ones((WINDOW, HEAD_DIM), BF16)
 
     def score_block(b, _):
@@ -254,21 +249,9 @@
 
     lax.fori_loop(0, BLOCKS, score_block, 0)
 
-    own[2].wait()
-    for copy in sends[2]:
-        copy.wait_recv()
+    wait_for(vbuf.at[pl.ds(PAD, ROWS)], in_recv.at[2])
     ones_row = jnp.ones((8, 2 * HEAD_DIM), BF16)
     row8 = lax.broadcasted_iota(jnp.int32, (8, TOK), 0)
-
-    def message_copy(owner):
-        return pltpu.make_async_remote_copy(
-            src_ref=message.at[owner],
-            dst_ref=gathered.at[me],
-            send_sem=msg_send.at[owner],
-            recv_sem=msg_recv.at[me],
-            device_id=(dp, owner),
-            device_id_type=MESH,
-        )
 
     def value_block(i, _):
         reach = (i + 1) // 2
@@ -298,92 +281,86 @@
 
             @pl.when(owner != me)
             def _():
-                message_copy(owner).start()
+                pltpu.make_async_remote_copy(
+                    src_ref=message.at[owner],
+                    dst_ref=gathered.at[me],
+                    send_sem=msg_send.at[0],
+                    recv_sem=msg_recv.at[0],
+                    device_id=(dp, owner),
+                    device_id_type=MESH,
+                ).start()
 
         return 0
 
     lax.fori_loop(0, BLOCKS, value_block, 0)
 
-    total = message[me].astype(F32)
-    for peer in peers:
-        pltpu.make_async_remote_copy(
-            src_ref=message.at[peer],
-            dst_ref=gathered.at[peer],
-            send_sem=msg_send.at[peer],
-            recv_sem=msg_recv.at[peer],
-            device_id=(dp, peer),
-            device_id_type=MESH,
-        ).wait_recv()
-        total = total + gathered[peer].astype(F32)
+    pltpu.make_async_copy(message.at[me], gathered.at[me], msg_recv.at[0]).start()
+    wait_for(gathered, msg_recv.at[0])
+    total = jnp.zeros((MSG, TOK), F32)
+    for head in range(N_SEQ):
+        total = total + gathered[head].astype(F32)
     center = (total[64:65] + total[65:66]) / WIDTH
     spread = (total[66:67] + total[67:68]) / WIDTH - center * center
     predicted = lax.rsqrt(spread + EPS) * (total[:CHANNELS] - center * btok[...]) + ctok[...]
     difference = predicted - target[...]
     error = jnp.sum(difference * difference, axis=0, keepdims=True) / CHANNELS
     mine = onehot[:, pl.ds(pl.multiple_of(me * TOK, TOK), TOK)]
-    partial = jnp.broadcast_to(jnp.sum(mine * error, axis=1, keepdims=True), (CLIPS, HEAD_DIM))
+    slot = lax.broadcasted_iota(jnp.int32, (CLIPS, HEAD_DIM), 0)
+    lanes = lax.broadcasted_iota(jnp.int32, (CLIPS, HEAD_DIM), 1)
+    partial = jnp.sum(mine * error, axis=1, keepdims=True)
+    partial = jnp.sum(jnp.where(slot == lanes, partial, 0.0), axis=0, keepdims=True)
     part_out[...] = partial
-    parts = []
-    for j, peer in enumerate(peers):
-        copy = pltpu.make_async_remote_copy(
+    for peer in reversed(peers):
+        pltpu.make_async_remote_copy(
             src_ref=part_out,
-            dst_ref=part_in.at[j],
-            send_sem=part_send.at[j],
-            recv_sem=part_recv.at[j],
+            dst_ref=part_in.at[me],
+            send_sem=part_send.at[0],
+            recv_sem=part_recv.at[0],
             device_id=(dp, peer),
             device_id_type=MESH,
-        )
-        copy.start()
-        parts.append(copy)
-    for j, copy in enumerate(parts):
-        copy.wait_recv()
-        partial = partial + part_in[j]
-    losses = partial / size_col
+        ).start()
+    part_in[me] = partial
+    wait_for(part_in.at[pl.ds(0, N_SEQ - 1)], part_recv.at[0])
+    partial = part_in[0]
+    for rank in range(1, N_SEQ):
+        partial = partial + part_in[rank]
+    losses = partial / size_row
     loss_out[...] = losses
-    lefts = []
     for i in range(1, N_DP):
-        copy = pltpu.make_async_remote_copy(
+        pltpu.make_async_remote_copy(
             src_ref=loss_out,
-            dst_ref=loss_in.at[i],
-            send_sem=loss_send.at[i],
-            recv_sem=loss_recv.at[i],
+            dst_ref=loss_in.at[dp],
+            send_sem=loss_send.at[0],
+            recv_sem=loss_recv.at[0],
             device_id=(lax.rem(dp + i, N_DP), me),
             device_id_type=MESH,
-        )
-        copy.start()
-        lefts.append(copy)
-    slot = lax.broadcasted_iota(jnp.int32, (CLIPS, HEAD_DIM), 0)
-    scores = jnp.where(slot + dp * CLIPS == order_lane, losses, 0.0)
-    for i in range(1, N_DP):
-        lefts[i - 1].wait_recv()
-        group = lax.rem(dp - i + N_DP, N_DP)
-        scores = scores + jnp.where(slot + group * CLIPS == order_lane, loss_in[i], 0.0)
-    out_ref[...] = jnp.sum(scores, axis=0, keepdims=True)
-
-    for row in sends:
-        for copy in row:
-            copy.wait_send()
-    for peer in peers:
-        message_copy(peer).wait_send()
-    for copy in parts:
-        copy.wait_send()
-    for copy in lefts:
-        copy.wait_send()
+        ).start()
+    loss_in[dp] = losses
+    wait_for(loss_in.at[pl.ds(0, N_DP - 1)], loss_recv.at[0])
+    scores = jnp.zeros((CLIPS, HEAD_DIM), F32)
+    for group in range(N_DP):
+        scores = scores + jnp.where(wanted == group * CLIPS, loss_in[group], 0.0)
+    scores = jnp.sum(scores, axis=1, keepdims=True)
+    out_ref[...] = jnp.sum(jnp.where(slot == lanes, scores, 0.0), axis=0, keepdims=True)
+
+    for t in range(3):
+        wait_for(qbuf.at[pl.ds(0, (N_SEQ - 1) * TOK)], in_send.at[t])
+    wait_for(message.at[pl.ds(0, N_SEQ - 1)], msg_send.at[0])
+    wait_for(part_in.at[pl.ds(0, N_SEQ - 1)], part_send.at[0])
+    wait_for(loss_in.at[pl.ds(0, N_DP - 1)], loss_send.at[0])
 
 
 def per_device(
     queries, keys, values, text_kv, text_lengths, clip_lengths, timesteps, mod_weight, final_weight, noise, clean, report_order
 ):
-    activated = jax.nn.silu(step_embedding(timesteps)).astype(BF16)
     text = text_kv.reshape(CLIPS, 2 * TEXT, HEAD_DIM)
     anywhere = pl.BlockSpec(memory_space=pl.ANY)
     vmem = pl.BlockSpec(memory_space=pltpu.VMEM)
-    smem = pl.BlockSpec(memory_space=pltpu.SMEM)
     dma = pltpu.SemaphoreType.DMA
     out = pl.pallas_call(
         kernel,
         out_shape=jax.ShapeDtypeStruct((1, HEAD_DIM), F32),
-        in_specs=[anywhere] * 4 + [vmem] + [smem] * 3 + [anywhere] * 4,
+        in_specs=[anywhere] * 12,
         out_specs=vmem,
         scratch_shapes=[
             pltpu.VMEM((ROWS, HEAD_DIM), BF16),
@@ -394,6 +371,10 @@
             pltpu.VMEM((CHANNELS, WIDTH), BF16),
             pltpu.VMEM((CHANNELS, TOK), F32),
             pltpu.VMEM((CHANNELS, TOK), F32),
+            pltpu.SMEM((CLIPS,), jnp.int32),
+            pltpu.SMEM((1, CLIPS), jnp.int32),
+            pltpu.SMEM((CLIPS,), jnp.int32),
+            pltpu.SMEM((CLIPS,), jnp.int32),
             pltpu.VMEM((CLIPS * TEXT, HEAD_DIM), BF16),
             pltpu.VMEM((CLIPS * TEXT, HEAD_DIM), BF16),
             pltpu.VMEM((ROWS, HEAD_DIM), BF16),
@@ -412,26 +393,25 @@
             pltpu.VMEM((ROWS, WINDOW), BF16),
             pltpu.VMEM((N_SEQ, MSG, TOK), BF16),
             pltpu.VMEM((N_SEQ, MSG, TOK), BF16),
-            pltpu.VMEM((CLIPS, HEAD_DIM), F32),
-            pltpu.VMEM((N_SEQ, CLIPS, HEAD_DIM), F32),
-            pltpu.VMEM((CLIPS, HEAD_DIM), F32),
-            pltpu.VMEM((N_DP, CLIPS, HEAD_DIM), F32),
-            dma((3, N_SEQ)),
-            dma((3, N_SEQ)),
+            pltpu.VMEM((1, HEAD_DIM), F32),
+            pltpu.VMEM((N_SEQ, 1, HEAD_DIM), F32),
+            pltpu.VMEM((1, HEAD_DIM), F32),
+            pltpu.VMEM((N_DP, 1, HEAD_DIM), F32),
+            dma((9,)),
             dma((3,)),
-            dma((5,)),
-            dma((N_SEQ,)),
-            dma((N_SEQ,)),
-            dma((N_SEQ,)),
-            dma((N_SEQ,)),
-            dma((N_DP,)),
-            dma((N_DP,)),
+            dma((3,)),
+            dma((1,)),
+            dma((1,)),
+            dma((1,)),
+            dma((1,)),
+            dma((1,)),
+            dma((1,)),
         ],
         compiler_params=pltpu.CompilerParams(
             collective_id=0, has_side_effects=True, vmem_limit_bytes=60 * 1024 * 1024
         ),
     )(
-        queries, keys, values, text, activated, text_lengths, clip_lengths, report_order, mod_weight, final_weight.T, noise.T, clean.T
+        queries, keys, values, text, text_lengths, clip_lengths, report_order, timesteps, mod_weight, final_weight.T, noise.T, clean.T
     )
     return out[0, :CLIPS]
 

time: 78.4 us -> 73.6 us (0.939)
  Pallas kernels: 75.6 us -> 72.3 us
  other arithmetic: 1.39 us -> 0 us
    pallas_call x1, Pallas kernels: 75.6 us -> 72.3 us  [per_device(): pl.pallas_call(kernel, out_shape=jax.ShapeDtypeStruct((1, HEAD_DIM), F32)...]
    convert_element_type x2 -> x0, other arithmetic: 1.27 us -> none  [the longest x1 0.66 us: step_embedding(): angles = timesteps.astype(F32)[:, None] * frequency[None, :]]
where the time goes in v2:
time: 73.6 us; the launch traced here: 73.5 us
  Pallas kernels  72.3 us (98%)
  local copies, waits for them, and re-layouts  1.19 us (2%)
    pallas_call x1, Pallas kernels, per_device(): pl.pallas_call(kernel, out_shape=jax.ShapeDtypeStruct((1, HEAD_DIM), F32)...  72.3 us

profile of v2, /device:TPU:1, one launch (start us, length us, event | category | flops | bytes accessed | tf_op | source)
XLA Modules:
  0.0 73.5 jit_solution(7314928369944761020)
XLA Ops:
  0.0 72.3 %shard_map.118 = f32[1,128]{1,0:T(1,128)} custom-call(bf16[128,2048]{1,0:T(8,128)(2,1)} %q_hbm.1, bf16[128,2048]{1,0:T(8,128)(2,1)} %k_hbm.1, bf16[128,2048]{1,0:T(8,128)(2,1)} %v_hbm.1, bf16[8,512,128]{2,1,0:T(8,128)(2,1)} %bitcast.6, s32[8]{0:T(128)} %tlen_hbm.1, s32[1,8]{1,0:T(1,128)} %clen_hbm.1, s32[8]{0:T(128)} %order_hbm.1, s32[8]{0:T(128)} %time_hbm.1, ...), custom_call_target="tpu_custom_call" | custom-call | tf_op jit(solution)/shard_map/pallas_call | solution.py:360
  72.3 1.2 %slice_bitcast_fusion = f32[8]{0:T(128)} fusion(f32[1,128]{1,0:T(1,128)} %shard_map.118), kind=kLoop, calls=%fused_computation | loop fusion | bytes 64 | tf_op jit(solution)/shard_map/squeeze | solution.py:416

commit v3 on v2

--- a/solution.py
+++ b/solution.py
@@ -60,7 +60,17 @@
 
 
 PARTNERS = [(0, 1), (1, 0), (-1, 0), (1, 1), (-1, 1), (2, 0), (-2, 0), (2, 1), (-2, 1)]
+NEAR = len(PARTNERS)
 PARTNERS += [(3, 0), (-3, 0), (3, 1), (-3, 1), (4, 0), (4, 1)]
+
+
+GROUPS = sorted(
+    [(dx, dy) for dx in range(4) for dy in range(8) if dx or dy],
+    key=lambda step: -(min(step[0], 4 - step[0]) + min(step[1], 8 - step[1])),
+)
+SOURCES = [0, 4, 3, -3, 2, -2, 1, -1]
+EARLY = 6
+FINISH = [4, 3, -3, 2, -2, 1, -1, 0]
 
 
 def wait_for(buffer, sem):
@@ -72,8 +82,8 @@
     out_ref,
     qbuf, kbuf, vbuf, textbuf, modw, finw, noise, clean, tlen_ref, clen_ref, order_ref, time_ref,
     tk, tv, qbias, kbias, tbias, onehot, clip_row, wall, btok, ctok, target,
-    text_max, text_sum, text_out, inverse, weights, message, gathered, part_out, part_in, loss_out, loss_in,
-    load_sem, in_send, in_recv, msg_send, msg_recv, part_send, part_recv, loss_send, loss_recv,
+    text_max, text_sum, text_out, inverse, weights, mixed_out, pair, taken, message, gathered, part_out, part_in, loss_out, loss_in,
+    far_sem, cross_sem, load_sem, in_send, in_recv, value_recv, pair_send, pair_recv, msg_send, msg_recv, part_send, part_recv, loss_send, loss_recv,
 ):
     me = lax.axis_index("seq")
     dp = lax.axis_index("dp")
@@ -82,10 +92,12 @@
     peers = [lax.rem(z + dz + 8, 8) * 2 + lax.rem(core + dc, 2) for dz, dc in PARTNERS]
 
     barrier = pltpu.get_barrier_semaphore()
-    for peer in peers:
+    for peer in peers[:NEAR]:
         pl.semaphore_signal(barrier, inc=1, device_id=(dp, peer), device_id_type=MESH)
-    for i in range(1, N_DP):
-        pl.semaphore_signal(barrier, inc=1, device_id=(lax.rem(dp + i, N_DP), me), device_id_type=MESH)
+    across = [lax.rem(dp // 8 + i, 4) * 8 + lax.rem(dp, 8) for i in range(1, 4)]
+    down = [dp // 8 * 8 + lax.rem(lax.rem(dp, 8) + i, 8) for i in range(1, 8)]
+    for group in across + down:
+        pl.semaphore_signal(barrier, inc=1, device_id=(group, me), device_id_type=MESH)
 
     loads = [
         pltpu.make_async_copy(src, dst, load_sem.at[i])
@@ -102,21 +114,35 @@
     streams = [(q_hbm, qbuf, 0), (k_hbm, kbuf, PAD), (v_hbm, vbuf, PAD)]
     for t, (src, dst, base) in enumerate(streams):
         pltpu.make_async_copy(
-            src.at[:, pl.ds(head_at, HEAD_DIM)], dst.at[pl.ds(pl.multiple_of(base + me * TOK, TOK), TOK)], in_recv.at[t]
+            src.at[:, pl.ds(head_at, HEAD_DIM)],
+            dst.at[pl.ds(pl.multiple_of(base + me * TOK, TOK), TOK)],
+            in_recv.at[t] if t < 2 else value_recv.at[0],
         ).start()
 
-    pl.semaphore_wait(barrier, N_SEQ - 1 + N_DP - 1)
-
-    for t, (src, dst, base) in enumerate(streams):
-        for peer in reversed(peers):
+    pl.semaphore_wait(barrier, NEAR + len(across) + len(down))
+    for dz in (2, -2):
+        pl.semaphore_signal(far_sem, inc=1, device_id=(dp, lax.rem(z + dz + 8, 8) * 2 + core), device_id_type=MESH)
+    for group in across:
+        pl.semaphore_signal(cross_sem, inc=1, device_id=(group, me), device_id_type=MESH)
+
+    def send_part(t, partners):
+        src, dst, base = streams[t]
+        for dz, dc in partners:
+            peer = lax.rem(z + dz + 8, 8) * 2 + lax.rem(core + dc, 2)
             pltpu.make_async_remote_copy(
                 src_ref=src.at[:, pl.ds(pl.multiple_of(peer * HEAD_DIM, HEAD_DIM), HEAD_DIM)],
                 dst_ref=dst.at[pl.ds(pl.multiple_of(base + me * TOK, TOK), TOK)],
                 send_sem=in_send.at[t],
-                recv_sem=in_recv.at[t],
+                recv_sem=in_recv.at[t] if t < 2 else value_recv.at[dz % 8],
                 device_id=(dp, peer),
                 device_id_type=MESH,
             ).start()
+
+    send_part(0, PARTNERS[:NEAR][::-1])
+    pl.semaphore_wait(far_sem, 2)
+    send_part(0, PARTNERS[NEAR:][::-1])
+    send_part(1, PARTNERS[::-1])
+    send_part(2, PARTNERS[::-1])
     for load in loads[:4]:
         load.wait()
 
@@ -229,7 +255,6 @@
     lax.fori_loop(0, BLOCKS, text_block, 0)
 
     wait_for(kbuf.at[pl.ds(PAD, ROWS)], in_recv.at[1])
-    one_wide = jnp.ones((WINDOW, HEAD_DIM), BF16)
 
     def score_block(b, _):
         rows = pl.ds(pl.multiple_of(b * BLOCK, BLOCK), BLOCK)
@@ -239,66 +264,122 @@
         scores = nt_dot(left, right)
         before = text_max[rows, :]
         top = jnp.maximum(before, jnp.max(scores, axis=1, keepdims=True))
-        weight = jnp.exp2((scores - top[:, :1]) * SCALE).astype(BF16)
-        weights[rows, :] = weight
+        weight = jnp.exp2((scores - top[:, :1]) * SCALE)
+        video_sum = jnp.sum(weight, axis=1, keepdims=True)
+        weight = weight.astype(BF16)
+        for t in range(5):
+            weights[b + t, pl.ds((4 - t) * BLOCK, BLOCK), :] = weight[:, t * BLOCK : (t + 1) * BLOCK]
         fade = jnp.exp2((before - top) * SCALE)
-        inv = 1.0 / (nn_dot(weight, one_wide) + text_sum[rows, :] * fade)
+        inv = 1.0 / (video_sum + text_sum[rows, :] * fade)
         inverse[rows, :] = inv
         text_out[rows, :] = text_out[rows, :] * (fade * inv)
         return 0
 
-    lax.fori_loop(0, BLOCKS, score_block, 0)
-
-    wait_for(vbuf.at[pl.ds(PAD, ROWS)], in_recv.at[2])
-    ones_row = jnp.ones((8, 2 * HEAD_DIM), BF16)
-    row8 = lax.broadcasted_iota(jnp.int32, (8, TOK), 0)
-
-    def value_block(i, _):
-        reach = (i + 1) // 2
-        step = 4 + reach - 2 * reach * lax.rem(i, 2)
-        b = lax.rem(z + step, 8)
+    lax.fori_loop(0, BLOCKS, score_block, 0, unroll=2)
+
+    mixed_out[...] = jnp.zeros(mixed_out.shape, F32)
+
+    def value_rows(dz):
+        chip = lax.rem(z - dz + 8, 8)
+        wait_for(vbuf.at[pl.ds(PAD, BLOCK)], value_recv.at[dz % 8])
+        return chip, vbuf[pl.ds(pl.multiple_of(PAD + chip * BLOCK, BLOCK), BLOCK), :]
+
+    def add_source(dz):
+        chip, rows = value_rows(dz)
+        around = pl.ds(pl.multiple_of(chip * BLOCK, BLOCK), 5 * BLOCK)
+        mixed_out[around, :] = mixed_out[around, :] + nn_dot(weights[chip + 2], rows)
+
+    ones_rows = jnp.ones((16, HEAD_DIM), BF16)
+    zero_rows = jnp.zeros((16, HEAD_DIM), BF16)
+    count_left = jnp.concatenate([ones_rows, zero_rows], axis=1)
+    count_both = jnp.concatenate([ones_rows, ones_rows], axis=1)
+    row16 = lax.broadcasted_iota(jnp.int32, (16, TOK), 0)
+    wide16 = lax.broadcasted_iota(jnp.int32, (16, BLOCK), 0)
+
+    def stat_rows(place, total, squares):
+        total_high, total_low = [x.astype(F32) for x in pieces(total, 2)]
+        square_high, square_low = [x.astype(F32) for x in pieces(squares, 2)]
+        rows = jnp.where(place == 2, square_high, jnp.where(place == 3, square_low, 0.0))
+        return jnp.where(place == 0, total_high, jnp.where(place == 1, total_low, rows))
+
+    def project(b):
         rows = pl.ds(pl.multiple_of(b * BLOCK, BLOCK), BLOCK)
-        window = pl.ds(pl.multiple_of(b * BLOCK, BLOCK), WINDOW)
         first = b // 2
-        mixed = nn_dot(weights[rows, :], vbuf[window, :])
+        mixed = mixed_out[pl.ds(pl.multiple_of((b + 2) * BLOCK, BLOCK), BLOCK), :]
         attended = (mixed * inverse[rows, :] + text_out[rows, :]).astype(BF16)
         fold = wall[pl.ds(pl.multiple_of(first * CHANNELS, CHANNELS), NEAR_CLIPS * CHANNELS), :]
-        for half in range(2):
-            owner = 2 * b + half
-            part = attended[half * TOK : (half + 1) * TOK]
-            spread = nt_dot(fold, jnp.concatenate([part, part], axis=1))
-            picked = jnp.zeros((CHANNELS, TOK), F32)
-            clip_here = clip_row[0:1, pl.ds(pl.multiple_of(owner * TOK, TOK), TOK)]
-            for j in range(NEAR_CLIPS):
-                picked = jnp.where(clip_here == first + j, spread[j * CHANNELS : (j + 1) * CHANNELS], picked)
-            wide_part = part.astype(F32)
-            total = nt_dot(ones_row[:, :HEAD_DIM], part)
-            squares = nt_dot(ones_row, jnp.concatenate(pieces(wide_part * wide_part, 2), axis=1))
-            total_high, total_low = [x.astype(F32) for x in pieces(total, 2)]
-            square_high, square_low = [x.astype(F32) for x in pieces(squares, 2)]
-            stats = jnp.where(row8 == 0, total_high, jnp.where(row8 == 1, total_low, jnp.where(row8 == 2, square_high, square_low)))
-            message[owner] = jnp.concatenate([picked, stats, jnp.zeros((8, TOK), F32)], axis=0).astype(BF16)
-
-            @pl.when(owner != me)
-            def _():
-                pltpu.make_async_remote_copy(
-                    src_ref=message.at[owner],
-                    dst_ref=gathered.at[me],
-                    send_sem=msg_send.at[0],
-                    recv_sem=msg_recv.at[0],
-                    device_id=(dp, owner),
-                    device_id_type=MESH,
-                ).start()
-
-        return 0
-
-    lax.fori_loop(0, BLOCKS, value_block, 0)
-
-    pltpu.make_async_copy(message.at[me], gathered.at[me], msg_recv.at[0]).start()
-    wait_for(gathered, msg_recv.at[0])
-    total = jnp.zeros((MSG, TOK), F32)
-    for head in range(N_SEQ):
-        total = total + gathered[head].astype(F32)
+        spread = nt_dot(jnp.concatenate([fold, count_left], axis=0), jnp.concatenate([attended, attended], axis=1))
+        clip_here = clip_row[0:1, rows]
+        picked = spread[:CHANNELS]
+        for j in range(1, NEAR_CLIPS):
+            picked = jnp.where(clip_here == first + j, spread[j * CHANNELS : (j + 1) * CHANNELS], picked)
+        wide = attended.astype(F32)
+        squares = nt_dot(count_both, jnp.concatenate(pieces(wide * wide, 2), axis=1))
+        stats = stat_rows(wide16, spread[NEAR_CLIPS * CHANNELS :], squares)
+        full = jnp.concatenate([picked, stats], axis=0).astype(BF16)
+        pair[b, 0] = full[:, :TOK]
+        pair[b, 1] = full[:, TOK:]
+
+    def exchange(i, b):
+        copy = pltpu.make_async_remote_copy(
+            src_ref=pair.at[b, 1 - core],
+            dst_ref=taken.at[b],
+            send_sem=pair_send.at[0],
+            recv_sem=pair_recv.at[i],
+            device_id=(dp, z * 2 + 1 - core),
+            device_id_type=MESH,
+        )
+        copy.start()
+        return copy
+
+    def message_copy(source, slot, owner):
+        pltpu.make_async_remote_copy(
+            src_ref=source,
+            dst_ref=gathered.at[slot],
+            send_sem=msg_send.at[0],
+            recv_sem=msg_recv.at[0],
+            device_id=(dp, owner),
+            device_id_type=MESH,
+        ).start()
+
+    def deliver(i, b, copy):
+        copy.wait_recv()
+        both = pair[b, core].astype(F32) + taken[b].astype(F32)
+        stats = stat_rows(row16, both[64:65] + both[65:66], both[66:67] + both[67:68])
+        total = jnp.concatenate([both[:CHANNELS], stats], axis=0).astype(BF16)
+        if FINISH[i] == 0:
+            gathered[2 * z] = total
+            return
+        message[b] = total
+        message_copy(message.at[b], 2 * z, b * 2 + core)
+
+    def finish(i):
+        b = lax.rem(z + FINISH[i] + 8, 8)
+        project(b)
+        if abs(FINISH[i]) == 3:
+            for to in range(2):
+                message_copy(pair.at[b, to], me, b * 2 + to)
+            return None
+        return i, b, exchange(i, b)
+
+    for dz in SOURCES[:EARLY]:
+        add_source(dz)
+    waiting = [finish(0)]
+    for dz in SOURCES[EARLY:]:
+        add_source(dz)
+    for i in range(1, len(FINISH)):
+        waiting.append(finish(i))
+    for entry in waiting:
+        if entry is not None:
+            deliver(*entry)
+
+    wait_for(gathered.at[pl.ds(0, 9)], msg_recv.at[0])
+    total = gathered[2 * z].astype(F32)
+    for dz in (1, 2, 3, 4, 5, 6, 7):
+        chip = lax.rem(z + dz, 8)
+        total = total + gathered[2 * chip].astype(F32)
+        if dz in (3, 5):
+            total = total + gathered[2 * chip + 1].astype(F32)
     center = (total[64:65] + total[65:66]) / WIDTH
     spread = (total[66:67] + total[67:68]) / WIDTH - center * center
     predicted = lax.rsqrt(spread + EPS) * (total[:CHANNELS] - center * btok[...]) + ctok[...]
@@ -325,14 +406,15 @@
     for rank in range(1, N_SEQ):
         partial = partial + part_in[rank]
     losses = partial / size_row
+    pl.semaphore_wait(cross_sem, len(across))
     loss_out[...] = losses
-    for i in range(1, N_DP):
+    for dx, dy in GROUPS:
         pltpu.make_async_remote_copy(
             src_ref=loss_out,
             dst_ref=loss_in.at[dp],
             send_sem=loss_send.at[0],
             recv_sem=loss_recv.at[0],
-            device_id=(lax.rem(dp + i, N_DP), me),
+            device_id=(lax.rem(dp // 8 + dx, 4) * 8 + lax.rem(dp % 8 + dy, 8), me),
             device_id_type=MESH,
         ).start()
     loss_in[dp] = losses
@@ -345,7 +427,8 @@
 
     for t in range(3):
         wait_for(qbuf.at[pl.ds(0, (N_SEQ - 1) * TOK)], in_send.at[t])
-    wait_for(message.at[pl.ds(0, N_SEQ - 1)], msg_send.at[0])
+    wait_for(taken.at[pl.ds(0, 6)], pair_send.at[0])
+    wait_for(gathered.at[pl.ds(0, 9)], msg_send.at[0])
     wait_for(part_in.at[pl.ds(0, N_SEQ - 1)], part_send.at[0])
     wait_for(loss_in.at[pl.ds(0, N_DP - 1)], loss_send.at[0])
 
@@ -390,16 +473,24 @@
             pltpu.VMEM((ROWS, HEAD_DIM), F32),
             pltpu.VMEM((ROWS, HEAD_DIM), F32),
             pltpu.VMEM((ROWS, HEAD_DIM), F32),
-            pltpu.VMEM((ROWS, WINDOW), BF16),
-            pltpu.VMEM((N_SEQ, MSG, TOK), BF16),
+            pltpu.VMEM((12, 5 * BLOCK, BLOCK), BF16),
+            pltpu.VMEM((12 * BLOCK, HEAD_DIM), F32),
+            pltpu.VMEM((8, 2, MSG, TOK), BF16),
+            pltpu.VMEM((8, MSG, TOK), BF16),
+            pltpu.VMEM((8, MSG, TOK), BF16),
             pltpu.VMEM((N_SEQ, MSG, TOK), BF16),
             pltpu.VMEM((1, HEAD_DIM), F32),
             pltpu.VMEM((N_SEQ, 1, HEAD_DIM), F32),
             pltpu.VMEM((1, HEAD_DIM), F32),
             pltpu.VMEM((N_DP, 1, HEAD_DIM), F32),
+            pltpu.SemaphoreType.REGULAR,
+            pltpu.SemaphoreType.REGULAR,
             dma((9,)),
             dma((3,)),
-            dma((3,)),
+            dma((2,)),
+            dma((8,)),
+            dma((1,)),
+            dma((8,)),
             dma((1,)),
             dma((1,)),
             dma((1,)),

time: 73.6 us -> 72.1 us (0.980)
  Pallas kernels: 72.3 us -> 70.8 us
    pallas_call x1, Pallas kernels: 72.3 us -> 70.8 us  [per_device(): pl.pallas_call(kernel, out_shape=jax.ShapeDtypeStruct((1, HEAD_DIM), F32)...]
where the time goes in v3:
time: 72.1 us; the launch traced here: 72 us
  Pallas kernels  70.8 us (98%)
  local copies, waits for them, and re-layouts  1.19 us (2%)
    pallas_call x1, Pallas kernels, per_device(): pl.pallas_call(kernel, out_shape=jax.ShapeDtypeStruct((1, HEAD_DIM), F32)...  70.8 us

profile of v3, /device:TPU:1, one launch (start us, length us, event | category | flops | bytes accessed | tf_op | source)
XLA Modules:
  0.0 72.0 jit_solution(7107471900778804721)
XLA Ops:
  0.0 70.8 %shard_map.118 = f32[1,128]{1,0:T(1,128)} custom-call(bf16[128,2048]{1,0:T(8,128)(2,1)} %q_hbm.1, bf16[128,2048]{1,0:T(8,128)(2,1)} %k_hbm.1, bf16[128,2048]{1,0:T(8,128)(2,1)} %v_hbm.1, bf16[8,512,128]{2,1,0:T(8,128)(2,1)} %bitcast.6, s32[8]{0:T(128)} %tlen_hbm.1, s32[1,8]{1,0:T(1,128)} %clen_hbm.1, s32[8]{0:T(128)} %order_hbm.1, s32[8]{0:T(128)} %time_hbm.1, ...), custom_call_target="tpu_custom_call" | custom-call | tf_op jit(solution)/shard_map/pallas_call | solution.py:443
  70.8 1.2 %slice_bitcast_fusion = f32[8]{0:T(128)} fusion(f32[1,128]{1,0:T(1,128)} %shard_map.118), kind=kLoop, calls=%fused_computation | loop fusion | bytes 64 | tf_op jit(solution)/shard_map/squeeze | solution.py:507

commit v4 on v3

--- a/solution.py
+++ b/solution.py
@@ -70,7 +70,7 @@
 )
 SOURCES = [0, 4, 3, -3, 2, -2, 1, -1]
 EARLY = 6
-FINISH = [4, 3, -3, 2, -2, 1, -1, 0]
+FINISH = [4, -3, 3, 2, -2, 1, -1, 0]
 
 
 def wait_for(buffer, sem):
@@ -94,11 +94,35 @@
     barrier = pltpu.get_barrier_semaphore()
     for peer in peers[:NEAR]:
         pl.semaphore_signal(barrier, inc=1, device_id=(dp, peer), device_id_type=MESH)
+    others = [lax.rem(dp // 8 + dx, 4) * 8 + lax.rem(lax.rem(dp, 8) + dy, 8) for dx, dy in GROUPS]
     across = [lax.rem(dp // 8 + i, 4) * 8 + lax.rem(dp, 8) for i in range(1, 4)]
     down = [dp // 8 * 8 + lax.rem(lax.rem(dp, 8) + i, 8) for i in range(1, 8)]
     for group in across + down:
         pl.semaphore_signal(barrier, inc=1, device_id=(group, me), device_id_type=MESH)
 
+    streams = [(q_hbm, qbuf, 0), (k_hbm, kbuf, PAD), (v_hbm, vbuf, PAD)]
+    pl.semaphore_wait(barrier, NEAR + len(across) + len(down))
+    for dz in (2, -2):
+        pl.semaphore_signal(far_sem, inc=1, device_id=(dp, lax.rem(z + dz + 8, 8) * 2 + core), device_id_type=MESH)
+    for group in across:
+        pl.semaphore_signal(cross_sem, inc=1, device_id=(group, me), device_id_type=MESH)
+
+    def send_part(t, partners):
+        src, dst, base = streams[t]
+        for dz, dc in partners:
+            peer = lax.rem(z + dz + 8, 8) * 2 + lax.rem(core + dc, 2)
+            pltpu.make_async_remote_copy(
+                src_ref=src.at[:, pl.ds(pl.multiple_of(peer * HEAD_DIM, HEAD_DIM), HEAD_DIM)],
+                dst_ref=dst.at[pl.ds(pl.multiple_of(base + me * TOK, TOK), TOK)],
+                send_sem=in_send.at[t],
+                recv_sem=in_recv.at[t] if t < 2 else value_recv.at[dz % 8],
+                device_id=(dp, peer),
+                device_id_type=MESH,
+            ).start()
+
+    send_part(0, PARTNERS[:NEAR][::-1])
+    pl.semaphore_wait(far_sem, 2)
+    send_part(0, PARTNERS[NEAR:][::-1])
     loads = [
         pltpu.make_async_copy(src, dst, load_sem.at[i])
         for i, (src, dst) in enumerate(
@@ -111,7 +135,6 @@
     for load in loads:
         load.start()
     head_at = pl.multiple_of(me * HEAD_DIM, HEAD_DIM)
-    streams = [(q_hbm, qbuf, 0), (k_hbm, kbuf, PAD), (v_hbm, vbuf, PAD)]
     for t, (src, dst, base) in enumerate(streams):
         pltpu.make_async_copy(
             src.at[:, pl.ds(head_at, HEAD_DIM)],
@@ -119,28 +142,6 @@
             in_recv.at[t] if t < 2 else value_recv.at[0],
         ).start()
 
-    pl.semaphore_wait(barrier, NEAR + len(across) + len(down))
-    for dz in (2, -2):
-        pl.semaphore_signal(far_sem, inc=1, device_id=(dp, lax.rem(z + dz + 8, 8) * 2 + core), device_id_type=MESH)
-    for group in across:
-        pl.semaphore_signal(cross_sem, inc=1, device_id=(group, me), device_id_type=MESH)
-
-    def send_part(t, partners):
-        src, dst, base = streams[t]
-        for dz, dc in partners:
-            peer = lax.rem(z + dz + 8, 8) * 2 + lax.rem(core + dc, 2)
-            pltpu.make_async_remote_copy(
-                src_ref=src.at[:, pl.ds(pl.multiple_of(peer * HEAD_DIM, HEAD_DIM), HEAD_DIM)],
-                dst_ref=dst.at[pl.ds(pl.multiple_of(base + me * TOK, TOK), TOK)],
-                send_sem=in_send.at[t],
-                recv_sem=in_recv.at[t] if t < 2 else value_recv.at[dz % 8],
-                device_id=(dp, peer),
-                device_id_type=MESH,
-            ).start()
-
-    send_part(0, PARTNERS[:NEAR][::-1])
-    pl.semaphore_wait(far_sem, 2)
-    send_part(0, PARTNERS[NEAR:][::-1])
     send_part(1, PARTNERS[::-1])
     send_part(2, PARTNERS[::-1])
     for load in loads[:4]:
@@ -356,7 +357,7 @@
     def finish(i):
         b = lax.rem(z + FINISH[i] + 8, 8)
         project(b)
-        if abs(FINISH[i]) == 3:
+        if abs(FINISH[i]) == 9:
             for to in range(2):
                 message_copy(pair.at[b, to], me, b * 2 + to)
             return None
@@ -365,20 +366,21 @@
     for dz in SOURCES[:EARLY]:
         add_source(dz)
     waiting = [finish(0)]
-    for dz in SOURCES[EARLY:]:
-        add_source(dz)
-    for i in range(1, len(FINISH)):
+    add_source(SOURCES[EARLY])
+    waiting.append(finish(1))
+    add_source(SOURCES[EARLY + 1])
+    for i in range(2, len(FINISH)):
         waiting.append(finish(i))
     for entry in waiting:
         if entry is not None:
             deliver(*entry)
 
-    wait_for(gathered.at[pl.ds(0, 9)], msg_recv.at[0])
+    wait_for(gathered.at[pl.ds(0, 7)], msg_recv.at[0])
     total = gathered[2 * z].astype(F32)
     for dz in (1, 2, 3, 4, 5, 6, 7):
         chip = lax.rem(z + dz, 8)
         total = total + gathered[2 * chip].astype(F32)
-        if dz in (3, 5):
+        if dz in ():
             total = total + gathered[2 * chip + 1].astype(F32)
     center = (total[64:65] + total[65:66]) / WIDTH
     spread = (total[66:67] + total[67:68]) / WIDTH - center * center
@@ -408,13 +410,13 @@
     losses = partial / size_row
     pl.semaphore_wait(cross_sem, len(across))
     loss_out[...] = losses
-    for dx, dy in GROUPS:
+    for group in others:
         pltpu.make_async_remote_copy(
             src_ref=loss_out,
             dst_ref=loss_in.at[dp],
             send_sem=loss_send.at[0],
             recv_sem=loss_recv.at[0],
-            device_id=(lax.rem(dp // 8 + dx, 4) * 8 + lax.rem(dp % 8 + dy, 8), me),
+            device_id=(group, me),
             device_id_type=MESH,
         ).start()
     loss_in[dp] = losses
@@ -427,8 +429,8 @@
 
     for t in range(3):
         wait_for(qbuf.at[pl.ds(0, (N_SEQ - 1) * TOK)], in_send.at[t])
-    wait_for(taken.at[pl.ds(0, 6)], pair_send.at[0])
-    wait_for(gathered.at[pl.ds(0, 9)], msg_send.at[0])
+    wait_for(taken.at[pl.ds(0, 8)], pair_send.at[0])
+    wait_for(gathered.at[pl.ds(0, 7)], msg_send.at[0])
     wait_for(part_in.at[pl.ds(0, N_SEQ - 1)], part_send.at[0])
     wait_for(loss_in.at[pl.ds(0, N_DP - 1)], loss_send.at[0])
 
@@ -499,11 +501,11 @@
             dma((1,)),
         ],
         compiler_params=pltpu.CompilerParams(
-            collective_id=0, has_side_effects=True, vmem_limit_bytes=60 * 1024 * 1024
+            collective_id=0, has_side_effects=True, vmem_limit_bytes=40 * 1024 * 1024
         ),
-    )(
+    )(*[pltpu.with_memory_space_constraint(operand, pltpu.HBM) for operand in (
         queries, keys, values, text, text_lengths, clip_lengths, report_order, timesteps, mod_weight, final_weight.T, noise.T, clean.T
-    )
+    )])
     return out[0, :CLIPS]
 
 

time: 72.1 us -> 70.7 us (0.981)
  Pallas kernels: 70.8 us -> 70 us
    pallas_call x1, Pallas kernels: 70.8 us -> 70 us  [per_device(): pl.pallas_call(kernel, out_shape=jax.ShapeDtypeStruct((1, HEAD_DIM), F32)...]
where the time goes in v4:
time: 70.7 us; the launch traced here: 70.5 us
  Pallas kernels  70 us (99%)
    pallas_call x1, Pallas kernels, per_device(): pl.pallas_call(kernel, out_shape=jax.ShapeDtypeStruct((1, HEAD_DIM), F32)...  70 us

profile of v4, /device:TPU:1, one launch (start us, length us, event | category | flops | bytes accessed | tf_op | source)
XLA Modules:
  0.0 70.5 jit_solution(14034223964593694920)
XLA Ops:
  0.0 70.0 %shard_map.118 = f32[1,128]{1,0:T(1,128)S(1)} custom-call(bf16[128,2048]{1,0:T(8,128)(2,1)} %q_hbm.1, bf16[128,2048]{1,0:T(8,128)(2,1)} %k_hbm.1, bf16[128,2048]{1,0:T(8,128)(2,1)} %v_hbm.1, bf16[8,512,128]{2,1,0:T(8,128)(2,1)} %bitcast.6, s32[8]{0:T(128)} %tlen_hbm.1, s32[1,8]{1,0:T(1,128)} %clen_hbm.1, s32[8]{0:T(128)} %order_hbm.1, s32[8]{0:T(128)} %time_hbm.1, ...), custom_call_target="tpu_custom_call" | custom-call | tf_op jit(solution)/shard_map/pallas_call | solution.py:445
  70.0 0.5 slice_bitcast_fusion

commit v5 on v4

--- a/solution.py
+++ b/solution.py
@@ -368,12 +368,12 @@
     waiting = [finish(0)]
     add_source(SOURCES[EARLY])
     waiting.append(finish(1))
+    deliver(*waiting[0])
     add_source(SOURCES[EARLY + 1])
     for i in range(2, len(FINISH)):
         waiting.append(finish(i))
-    for entry in waiting:
-        if entry is not None:
-            deliver(*entry)
+    for entry in waiting[1:]:
+        deliver(*entry)
 
     wait_for(gathered.at[pl.ds(0, 7)], msg_recv.at[0])
     total = gathered[2 * z].astype(F32)

time: 70.7 us -> 70.4 us (level)
  no operation moved by 1% of the time
where the time goes in v5:
time: 70.4 us; the launch traced here: 70.3 us
  Pallas kernels  69.8 us (99%)
    pallas_call x1, Pallas kernels, per_device(): pl.pallas_call(kernel, out_shape=jax.ShapeDtypeStruct((1, HEAD_DIM), F32)...  69.8 us

profile of v5, /device:TPU:1, one launch (start us, length us, event | category | flops | bytes accessed | tf_op | source)
XLA Modules:
  0.0 70.3 jit_solution(2925141931048972863)
XLA Ops:
  0.0 69.8 %shard_map.118 = f32[1,128]{1,0:T(1,128)S(1)} custom-call(bf16[128,2048]{1,0:T(8,128)(2,1)} %q_hbm.1, bf16[128,2048]{1,0:T(8,128)(2,1)} %k_hbm.1, bf16[128,2048]{1,0:T(8,128)(2,1)} %v_hbm.1, bf16[8,512,128]{2,1,0:T(8,128)(2,1)} %bitcast.6, s32[8]{0:T(128)} %tlen_hbm.1, s32[1,8]{1,0:T(1,128)} %clen_hbm.1, s32[8]{0:T(128)} %order_hbm.1, s32[8]{0:T(128)} %time_hbm.1, ...), custom_call_target="tpu_custom_call" | custom-call | tf_op jit(solution)/shard_map/pallas_call | solution.py:445
  69.8 0.5 slice_bitcast_fusion

commit v6 on v5

--- a/solution.py
+++ b/solution.py
@@ -298,10 +298,13 @@
     wide16 = lax.broadcasted_iota(jnp.int32, (16, BLOCK), 0)
 
     def stat_rows(place, total, squares):
-        total_high, total_low = [x.astype(F32) for x in pieces(total, 2)]
-        square_high, square_low = [x.astype(F32) for x in pieces(squares, 2)]
-        rows = jnp.where(place == 2, square_high, jnp.where(place == 3, square_low, 0.0))
-        return jnp.where(place == 0, total_high, jnp.where(place == 1, total_low, rows))
+        rows = jnp.zeros(place.shape, F32)
+        for at, piece in enumerate(pieces(total, 3) + pieces(squares, 3)):
+            rows = jnp.where(place == at, piece.astype(F32), rows)
+        return rows
+
+    def read_stats(rows):
+        return rows[64:65] + rows[65:66] + rows[66:67], rows[67:68] + rows[68:69] + rows[69:70]
 
     def project(b):
         rows = pl.ds(pl.multiple_of(b * BLOCK, BLOCK), BLOCK)
@@ -346,7 +349,7 @@
     def deliver(i, b, copy):
         copy.wait_recv()
         both = pair[b, core].astype(F32) + taken[b].astype(F32)
-        stats = stat_rows(row16, both[64:65] + both[65:66], both[66:67] + both[67:68])
+        stats = stat_rows(row16, *read_stats(both))
         total = jnp.concatenate([both[:CHANNELS], stats], axis=0).astype(BF16)
         if FINISH[i] == 0:
             gathered[2 * z] = total
@@ -357,10 +360,6 @@
     def finish(i):
         b = lax.rem(z + FINISH[i] + 8, 8)
         project(b)
-        if abs(FINISH[i]) == 9:
-            for to in range(2):
-                message_copy(pair.at[b, to], me, b * 2 + to)
-            return None
         return i, b, exchange(i, b)
 
     for dz in SOURCES[:EARLY]:
@@ -380,10 +379,9 @@
     for dz in (1, 2, 3, 4, 5, 6, 7):
         chip = lax.rem(z + dz, 8)
         total = total + gathered[2 * chip].astype(F32)
-        if dz in ():
-            total = total + gathered[2 * chip + 1].astype(F32)
-    center = (total[64:65] + total[65:66]) / WIDTH
-    spread = (total[66:67] + total[67:68]) / WIDTH - center * center
+    features, squares = read_stats(total)
+    center = features / WIDTH
+    spread = squares / WIDTH - center * center
     predicted = lax.rsqrt(spread + EPS) * (total[:CHANNELS] - center * btok[...]) + ctok[...]
     difference = predicted - target[...]
     error = jnp.sum(difference * difference, axis=0, keepdims=True) / CHANNELS

time: 70.4 us -> 70.5 us (level)
  no operation moved by 1% of the time
where the time goes in v6:
time: 70.5 us; the launch traced here: 70.3 us
  Pallas kernels  69.8 us (99%)
    pallas_call x1, Pallas kernels, per_device(): pl.pallas_call(kernel, out_shape=jax.ShapeDtypeStruct((1, HEAD_DIM), F32)...  69.8 us

profile of v6, /device:TPU:1, one launch (start us, length us, event | category | flops | bytes accessed | tf_op | source)
XLA Modules:
  0.0 70.3 jit_solution(25906923167242232)
XLA Ops:
  0.0 69.8 %shard_map.118 = f32[1,128]{1,0:T(1,128)S(1)} custom-call(bf16[128,2048]{1,0:T(8,128)(2,1)} %q_hbm.1, bf16[128,2048]{1,0:T(8,128)(2,1)} %k_hbm.1, bf16[128,2048]{1,0:T(8,128)(2,1)} %v_hbm.1, bf16[8,512,128]{2,1,0:T(8,128)(2,1)} %bitcast.6, s32[8]{0:T(128)} %tlen_hbm.1, s32[1,8]{1,0:T(1,128)} %clen_hbm.1, s32[8]{0:T(128)} %order_hbm.1, s32[8]{0:T(128)} %time_hbm.1, ...), custom_call_target="tpu_custom_call" | custom-call | tf_op jit(solution)/shard_map/pallas_call | solution.py:443
  69.8 0.5 slice_bitcast_fusion
